TPU v7x, 32 devices: a whole 2x2x4 slice. The times are simulated.
32 devices in a mesh: dp: 16 (over z, x, core), mp: 2 (over y).
Axes of the slice: x: 2, y: 2, z: 4, core: 2. Of those that a mesh axis runs over, the one named last changes fastest.
Arguments:
- tokens: bfloat16 [16, 1024, 768], P('dp'), may hold values from -6 to 6
- teacher_tokens: bfloat16 [16, 1024, 768], P('dp'), may hold values from -6 to 6
- cotangent: bfloat16 [16, 1024, 768], P('dp')
- lengths: int32 [16], P('dp'), may hold values from 256 to 1024, as said below
- masked: int32 [16, 128], P('dp'), may hold values from 0 to 1023, as said below
- attn_weight: float32 [3, 768, 768], P(None, 'dp', 'mp')
- out_weight: float32 [768, 768], P('mp', 'dp')
- up_weight: float32 [768, 3072], P('dp', 'mp')
- down_weight: float32 [3072, 768], P('mp', 'dp')
- attn_first: float32 [3, 768, 768], P(None, 'dp', 'mp')
- out_first: float32 [768, 768], P('mp', 'dp')
- up_first: float32 [768, 3072], P('dp', 'mp')
- down_first: float32 [3072, 768], P('mp', 'dp')
- attn_second: float32 [3, 768, 768], P(None, 'dp', 'mp'), may hold values from 1.024 to 4.096
- out_second: float32 [768, 768], P('mp', 'dp'), may hold values from 0.65536 to 2.62144
- up_second: float32 [768, 3072], P('dp', 'mp'), may hold values from 1.024 to 4.096
- down_second: float32 [3072, 768], P('mp', 'dp'), may hold values from 4.9152 to 19.6608
- vectors: float32 [9216], replicated, as said below
- vector_first: float32 [9216], replicated, may hold values from -64 to 64
- vector_second: float32 [9216], replicated, may hold values from 8.192 to 32.768
- teacher_attn: bfloat16 [3, 768, 768], P(None, 'dp', 'mp'), may hold values from -0.3125 to 0.3125
- teacher_out: bfloat16 [768, 768], P('mp', 'dp'), may hold values from -0.75 to 0.75
- teacher_up: bfloat16 [768, 3072], P('dp', 'mp'), may hold values from -0.21875 to 0.21875
- teacher_down: bfloat16 [3072, 768], P('mp', 'dp'), may hold values from -0.109375 to 0.109375
- teacher_vectors: bfloat16 [9216], replicated, as said below
Outputs:
- student_out: bfloat16 [16, 1024, 768], P('dp')
- input_grad: float32 [16, 1024, 768], P('dp')
- attn_updated: float32 [3, 768, 768], P(None, 'dp', 'mp')
- out_updated: float32 [768, 768], P('mp', 'dp')
- up_updated: float32 [768, 3072], P('dp', 'mp')
- down_updated: float32 [3072, 768], P('mp', 'dp')
- attn_moment: float32 [3, 768, 768], P(None, 'dp', 'mp')
- out_moment: float32 [768, 768], P('mp', 'dp')
- up_moment: float32 [768, 3072], P('dp', 'mp')
- down_moment: float32 [3072, 768], P('mp', 'dp')
- attn_square: float32 [3, 768, 768], P(None, 'dp', 'mp')
- out_square: float32 [768, 768], P('mp', 'dp')
- up_square: float32 [768, 3072], P('dp', 'mp')
- down_square: float32 [3072, 768], P('mp', 'dp')
- vector_moment: float32 [9216], replicated
- vector_square: float32 [9216], replicated
- vector_updated: float32 [9216], replicated
- matrix_norms: float32 [2, 6], replicated
- trust_ratios: float32 [6], replicated
Inputs may be any that keep to these rules, and one draw needn't show every extreme that they name: `lengths`: keys at or past a sequence's length are padding and take no attention; some sequence is full in every draw. `masked`: each position lies below its sequence's length; positions may repeat. `vectors`: gains near one, biases of either sign. `teacher_vectors`: gains near one, biases of either sign.
All inputs are finite; a program needn't handle non-finite values.
Results may differ from a plain program's by a relative error of at most 0.014.
The roundings to bfloat16 on the way count: a program that leaves them out, or rounds other values in their place, can miss the bound.
Values may be sent and summed in bfloat16 or wider, within the bound.
A program may use at most 128 MiB of HBM per device.

v0:
```python
from functools import partial

import jax
import jax.numpy as jnp
from jax import lax
from jax.sharding import PartitionSpec as P

HDIM = 64
STEP = 5


beta_one = 0.9
beta_two = 0.999
adam_eps = 1e-06
decay_rate = 0.01
matrix_rate = 0.3
vector_rate = 0.2
cosine_weight = 32.0
cosine_eps = 1e-06
layer_eps = 1e-12
masked_score = -1e30


def layer_norm(row_values, gain_vec, shift_vec):
    center = row_values - jnp.mean(row_values, -1, keepdims=True)
    spread = jnp.mean(center * center, -1, keepdims=True)
    return center * lax.rsqrt(spread + layer_eps) * gain_vec + shift_vec


def vector_parts(packed, model_width):
    pieces = [
        packed[position * model_width : (position + 1) * model_width] for position in range(8)
    ]
    return pieces + [packed[8 * model_width :]]


def row_share(term_fn, share_rows):
    return lax.psum_scatter(
        term_fn(jnp.int32(0), share_rows * lax.axis_size("mp")),
        "mp",
        scatter_dimension=0,
        tiled=True,
    )


def row_join_low(share_values):
    return lax.all_gather(share_values, "mp", axis=0, tiled=True)


def row_join(share_values):
    return lax.all_gather(share_values, "mp", axis=0, tiled=True)


def product_rows(left_rows, right_matrix):

    def term_fn(start, count):
        return jnp.dot(left_rows, right_matrix, preferred_element_type=jnp.float32)

    return term_fn


def split_heads(flat_rows, seq_count, length):
    return flat_rows.reshape(seq_count, length, flat_rows.shape[1] // HDIM, HDIM).transpose(
        2, 0, 1, 3
    )


def merge_heads(split_rows):
    head_count, seq_count, length, head_size = split_rows.shape
    return split_rows.transpose(1, 2, 0, 3).reshape(seq_count * length, head_count * head_size)


def head_scores(query, key_rows, visible):
    scale_factor = query.shape[-1] ** (-0.5)
    scores = (
        jnp.einsum("sqe,ske->sqk", query, key_rows, preferred_element_type=jnp.float32)
        * scale_factor
    )
    return jnp.where(visible[:, None, :], scores, masked_score)


def head_forward(query, key_rows, value_rows, visible):
    scores = head_scores(query, key_rows, visible)
    row_peak = jnp.max(scores, -1, keepdims=True)
    exponent = jnp.exp(scores - row_peak)
    row_total = jnp.sum(exponent, -1, keepdims=True)
    weights_low = (exponent / row_total).astype(jnp.bfloat16)
    mixed = jnp.einsum("sqk,ske->sqe", weights_low, value_rows, preferred_element_type=jnp.float32)
    return (mixed.astype(jnp.bfloat16), (row_peak + jnp.log(row_total))[..., 0])


def head_backward(query, key_rows, value_rows, grad_mixed, log_total, visible):
    scale_factor = query.shape[-1] ** (-0.5)
    scores = head_scores(query, key_rows, visible)
    probs = jnp.exp(scores - log_total[..., None])
    grad_probs = jnp.einsum(
        "sqe,ske->sqk", grad_mixed, value_rows, preferred_element_type=jnp.float32
    )
    inner = jnp.sum(probs * grad_probs, -1, keepdims=True)
    grad_scores = (probs * (grad_probs - inner)).astype(jnp.bfloat16)
    grad_query = (
        jnp.einsum("sqk,ske->sqe", grad_scores, key_rows, preferred_element_type=jnp.float32)
        * scale_factor
    ).astype(jnp.bfloat16)
    grad_keys = (
        jnp.einsum("sqk,sqe->ske", grad_scores, query, preferred_element_type=jnp.float32)
        * scale_factor
    ).astype(jnp.bfloat16)
    grad_values = jnp.einsum(
        "sqk,sqe->ske", probs.astype(jnp.bfloat16), grad_mixed, preferred_element_type=jnp.float32
    ).astype(jnp.bfloat16)
    return (grad_query, grad_keys, grad_values)


def forward_model(tokens, visible, weights, packed, shard_at, share_rows):
    attn_w, out_w, up_w, down_w = weights
    seq_count, length, model_width = tokens.shape
    local_width = attn_w.shape[2]
    hidden_local = up_w.shape[1]
    pieces = vector_parts(packed, model_width)
    bias_query = lax.dynamic_slice_in_dim(pieces[0], shard_at * local_width, local_width)
    bias_value = lax.dynamic_slice_in_dim(pieces[1], shard_at * local_width, local_width)
    bias_up = lax.dynamic_slice_in_dim(pieces[8], shard_at * hidden_local, hidden_local)
    row_values = tokens.reshape(seq_count * length, model_width)
    projected = jnp.einsum("rd,pde->pre", row_values, attn_w, preferred_element_type=jnp.float32)
    query_heads = split_heads((projected[0] + bias_query).astype(jnp.bfloat16), seq_count, length)
    key_heads = split_heads(projected[1].astype(jnp.bfloat16), seq_count, length)
    value_heads = split_heads((projected[2] + bias_value).astype(jnp.bfloat16), seq_count, length)
    mixed, log_total = lax.map(
        lambda grouped: head_forward(grouped[0], grouped[1], grouped[2], visible),
        (query_heads, key_heads, value_heads),
    )
    attended = merge_heads(mixed)
    share_start = shard_at * share_rows
    own_rows = lax.dynamic_slice_in_dim(row_values, share_start, share_rows, 0).astype(jnp.float32)
    first_sum = own_rows + row_share(product_rows(attended, out_w), share_rows) + pieces[2]
    normed = layer_norm(first_sum, pieces[3], pieces[4])
    normed_low = row_join_low(normed.astype(jnp.bfloat16))
    gate_in = jnp.dot(normed_low, up_w, preferred_element_type=jnp.float32) + bias_up
    activated = jax.nn.gelu(gate_in, approximate=False).astype(jnp.bfloat16)
    second_sum = normed + row_share(product_rows(activated, down_w), share_rows) + pieces[5]
    outcome = row_join(layer_norm(second_sum, pieces[6], pieces[7]))
    saved = (
        row_values,
        query_heads,
        key_heads,
        value_heads,
        log_total,
        attended,
        first_sum,
        normed_low,
        gate_in,
        activated,
        second_sum,
    )
    return (outcome, saved)


def adam_moments(grad_now, first_old, second_old):
    first_new = beta_one * first_old + (1.0 - beta_one) * grad_now
    second_new = beta_two * second_old + (1.0 - beta_two) * grad_now * grad_now
    step_now = (
        first_new
        / (1.0 - beta_one**STEP)
        / (jnp.sqrt(second_new / (1.0 - beta_two**STEP)) + adam_eps)
    )
    return (first_new, second_new, step_now)


def matrix_squares(attn_w, out_w, up_w, down_w):
    return jnp.concatenate(
        [
            jnp.sum(attn_w * attn_w, axis=(1, 2)),
            jnp.stack([jnp.sum(out_w * out_w), jnp.sum(up_w * up_w), jnp.sum(down_w * down_w)]),
        ]
    )


def local(
    tokens,
    teacher_tokens,
    cotangent,
    lengths,
    masked,
    attn_weight,
    out_weight,
    up_weight,
    down_weight,
    attn_first,
    out_first,
    up_first,
    down_first,
    attn_second,
    out_second,
    up_second,
    down_second,
    vectors,
    vector_first,
    vector_second,
    teacher_attn,
    teacher_out,
    teacher_up,
    teacher_down,
    teacher_vectors,
):
    shard_at = lax.axis_index("mp")
    leading = (shard_at == 0).astype(jnp.float32)
    seq_count, length, model_width = tokens.shape
    share_rows = seq_count * length // lax.axis_size("mp")
    share_start = shard_at * share_rows
    visible = jnp.arange(length)[None, :] < lengths[:, None]
    student = (
        lax.all_gather(attn_weight.astype(jnp.bfloat16), "dp", axis=1, tiled=True),
        lax.all_gather(out_weight.astype(jnp.bfloat16), "dp", axis=1, tiled=True),
        lax.all_gather(up_weight.astype(jnp.bfloat16), "dp", axis=0, tiled=True),
        lax.all_gather(down_weight.astype(jnp.bfloat16), "dp", axis=1, tiled=True),
    )
    teacher = (
        lax.all_gather(teacher_attn, "dp", axis=1, tiled=True),
        lax.all_gather(teacher_out, "dp", axis=1, tiled=True),
        lax.all_gather(teacher_up, "dp", axis=0, tiled=True),
        lax.all_gather(teacher_down, "dp", axis=1, tiled=True),
    )
    attn_w, out_w, up_w, down_w = student
    local_width = attn_w.shape[2]
    hidden_local = up_w.shape[1]
    teacher_rows, unused_saved = forward_model(
        teacher_tokens, visible, teacher, teacher_vectors.astype(jnp.float32), shard_at, share_rows
    )
    student_rows, saved = forward_model(tokens, visible, student, vectors, shard_at, share_rows)
    (
        row_values,
        query_heads,
        key_heads,
        value_heads,
        log_total,
        attended,
        first_sum,
        normed_low,
        gate_in,
        activated,
        second_sum,
    ) = saved
    student_out = student_rows.astype(jnp.bfloat16).reshape(seq_count, length, model_width)
    teacher_shaped = teacher_rows.reshape(seq_count, length, model_width)
    picks = masked[:, :, None]

    def loss_rows(outcome):
        shaped = outcome.reshape(seq_count, length, model_width)
        linear = jnp.sum(cotangent.astype(jnp.float32) * shaped)
        picked = jnp.take_along_axis(shaped, picks, axis=1)
        aimed = jnp.take_along_axis(teacher_shaped, picks, axis=1)
        inner = jnp.sum(picked * aimed, -1)
        scale_own = jnp.sqrt(jnp.sum(picked * picked, -1) + cosine_eps)
        scale_aim = jnp.sqrt(jnp.sum(aimed * aimed, -1) + cosine_eps)
        return linear + cosine_weight * jnp.sum(1.0 - inner / (scale_own * scale_aim))

    unused_loss, pull_loss = jax.vjp(loss_rows, student_rows)
    (grad_result,) = pull_loss(jnp.ones((), jnp.float32))
    pieces = vector_parts(vectors, model_width)
    grad_top = lax.dynamic_slice_in_dim(grad_result, share_start, share_rows, 0)
    gain_scale = 1.0
    unused_top, pull_top = jax.vjp(layer_norm, second_sum, pieces[6], pieces[7])
    grad_second, grad_gain_two, grad_shift_two = pull_top(grad_top)
    feed_low = grad_second.astype(jnp.bfloat16)
    feed_low = row_join_low(feed_low)
    grad_bias_down = jnp.sum(feed_low.astype(jnp.float32), 0)
    grad_down = jnp.einsum("rf,rd->fd", activated, feed_low, preferred_element_type=jnp.float32)
    grad_act = jnp.einsum("rd,fd->rf", feed_low, down_w, preferred_element_type=jnp.float32)
    unused_gelu, pull_gelu = jax.vjp(partial(jax.nn.gelu, approximate=False), gate_in)
    (grad_gate,) = pull_gelu(grad_act)
    gate_low = grad_gate.astype(jnp.bfloat16)
    grad_bias_up = jnp.sum(gate_low.astype(jnp.float32), 0)
    grad_up = jnp.einsum("rd,rf->df", normed_low, gate_low, preferred_element_type=jnp.float32)
    grad_normed = grad_second + row_share(product_rows(gate_low, up_w.T), share_rows)
    unused_mid, pull_mid = jax.vjp(layer_norm, first_sum, pieces[3], pieces[4])
    grad_first, grad_gain_one, grad_shift_one = pull_mid(grad_normed)
    branch_low = grad_first.astype(jnp.bfloat16)
    branch_low = row_join_low(branch_low)
    grad_bias_out = jnp.sum(branch_low.astype(jnp.float32), 0)
    grad_out = jnp.einsum("rh,rd->hd", attended, branch_low, preferred_element_type=jnp.float32)
    grad_attended = jnp.einsum(
        "rd,hd->rh", branch_low, out_w, preferred_element_type=jnp.float32
    ).astype(jnp.bfloat16)
    grad_heads = split_heads(grad_attended, seq_count, length)
    grad_query, grad_keys, grad_values = lax.map(
        lambda grouped: head_backward(
            grouped[0], grouped[1], grouped[2], grouped[3], grouped[4], visible
        ),
        (query_heads, key_heads, value_heads, grad_heads, log_total),
    )
    grad_projected = jnp.stack(
        [merge_heads(grad_query), merge_heads(grad_keys), merge_heads(grad_values)]
    )
    grad_attn = jnp.einsum(
        "rd,pre->pde", row_values, grad_projected, preferred_element_type=jnp.float32
    )
    summed_attn, summed_out, summed_up, summed_down = (
        lax.psum_scatter(grad_attn, "dp", scatter_dimension=1, tiled=True),
        lax.psum_scatter(grad_out, "dp", scatter_dimension=1, tiled=True),
        lax.psum_scatter(grad_up, "dp", scatter_dimension=0, tiled=True),
        lax.psum_scatter(grad_down, "dp", scatter_dimension=1, tiled=True),
    )

    def input_term(start, count):
        return jnp.einsum("pre,pde->rd", grad_projected, attn_w, preferred_element_type=jnp.float32)

    input_grad = row_join(grad_first + row_share(input_term, share_rows)).reshape(
        seq_count, length, model_width
    )
    grad_bias_query = jnp.sum(grad_projected[0].astype(jnp.float32), 0)
    grad_bias_value = jnp.sum(grad_projected[2].astype(jnp.float32), 0)
    zeros_model = jnp.zeros((model_width,), jnp.float32)
    zeros_hidden = jnp.zeros((pieces[8].shape[0],), jnp.float32)
    vector_grad = jnp.concatenate(
        [
            lax.dynamic_update_slice_in_dim(
                zeros_model, grad_bias_query, shard_at * local_width, 0
            ),
            lax.dynamic_update_slice_in_dim(
                zeros_model, grad_bias_value, shard_at * local_width, 0
            ),
            leading * grad_bias_out,
            gain_scale * grad_gain_one,
            gain_scale * grad_shift_one,
            leading * grad_bias_down,
            gain_scale * grad_gain_two,
            gain_scale * grad_shift_two,
            lax.dynamic_update_slice_in_dim(zeros_hidden, grad_bias_up, shard_at * hidden_local, 0),
        ]
    )
    attn_moment, attn_square, step_attn = adam_moments(summed_attn, attn_first, attn_second)
    out_moment, out_square, step_out = adam_moments(summed_out, out_first, out_second)
    up_moment, up_square, step_up = adam_moments(summed_up, up_first, up_second)
    down_moment, down_square, step_down = adam_moments(summed_down, down_first, down_second)
    step_attn = step_attn + decay_rate * attn_weight
    step_out = step_out + decay_rate * out_weight
    step_up = step_up + decay_rate * up_weight
    step_down = step_down + decay_rate * down_weight
    update_squares = matrix_squares(step_attn, step_out, step_up, step_down)
    weight_total, update_total, vector_total = lax.psum(
        (
            matrix_squares(attn_weight, out_weight, up_weight, down_weight),
            update_squares,
            vector_grad,
        ),
        ("dp", "mp"),
    )
    weight_norms = jnp.sqrt(weight_total)
    update_norms = jnp.sqrt(update_total)
    trust_ratio = weight_norms / update_norms
    attn_updated = attn_weight - matrix_rate * trust_ratio[0:3][:, None, None] * step_attn
    out_updated = out_weight - matrix_rate * trust_ratio[3] * step_out
    up_updated = up_weight - matrix_rate * trust_ratio[4] * step_up
    down_updated = down_weight - matrix_rate * trust_ratio[5] * step_down
    vector_moment, vector_square, step_vector = adam_moments(
        vector_total, vector_first, vector_second
    )
    vector_updated = vectors - vector_rate * step_vector
    return (
        student_out,
        input_grad,
        attn_updated,
        out_updated,
        up_updated,
        down_updated,
        attn_moment,
        out_moment,
        up_moment,
        down_moment,
        attn_square,
        out_square,
        up_square,
        down_square,
        vector_moment,
        vector_square,
        vector_updated,
        jnp.stack([weight_norms, update_norms]),
        trust_ratio,
    )


def solution(mesh):
    return jax.shard_map(
        local,
        mesh=mesh,
        in_specs=(
            P("dp", None, None),
            P("dp", None, None),
            P("dp", None, None),
            P("dp"),
            P("dp", None),
            P(None, "dp", "mp"),
            P("mp", "dp"),
            P("dp", "mp"),
            P("mp", "dp"),
            P(None, "dp", "mp"),
            P("mp", "dp"),
            P("dp", "mp"),
            P("mp", "dp"),
            P(None, "dp", "mp"),
            P("mp", "dp"),
            P("dp", "mp"),
            P("mp", "dp"),
            P(),
            P(),
            P(),
            P(None, "dp", "mp"),
            P("mp", "dp"),
            P("dp", "mp"),
            P("mp", "dp"),
            P(),
        ),
        out_specs=(
            P("dp", None, None),
            P("dp", None, None),
            P(None, "dp", "mp"),
            P("mp", "dp"),
            P("dp", "mp"),
            P("mp", "dp"),
            P(None, "dp", "mp"),
            P("mp", "dp"),
            P("dp", "mp"),
            P("mp", "dp"),
            P(None, "dp", "mp"),
            P("mp", "dp"),
            P("dp", "mp"),
            P("mp", "dp"),
            P(),
            P(),
            P(),
            P(),
            P(),
        ),
        check_vma=False,
    )
```

profile of v0, /device:TPU:0, one launch (start us, length us, event | category | flops | bytes accessed | tf_op | source)
XLA Modules:
  0.0 1255.5 jit_solution(535330406119069810)
XLA Ops:
  14.0 27.0 %all_gather.52 = bf16[384,768]{0,1:T(8,128)(2,1)} all-gather(bf16[384,48]{0,1:T(8,128)(2,1)} %param.52), channel_id=1, replica_groups=mesh['dp'=16,'mp'=2] {'dp'}, dimensions={1}, use_global_device_ids=true | all-gather | bytes 626688 | tf_op jit(solution)/shard_map/all_gather | solution.py:220
  41.0 21.8 %all_gather.46 = bf16[384,768]{0,1:T(8,128)(2,1)} all-gather(bf16[384,48]{0,1:T(8,128)(2,1)S(1)} %convert_element_type.181), channel_id=1, replica_groups=mesh['dp'=16,'mp'=2] {'dp'}, dimensions={1}, use_global_device_ids=true | all-gather | bytes 626688 | tf_op jit(solution)/shard_map/all_gather | solution.py:214
  62.8 4.0 convolution_bitcast_fusion
  69.7 29.3 %all-gather.14.cloned.1.call-done = bf16[3,768,384]{2,1,0:T(8,128)(2,1)} async-done(((bf16[3,48,384]{2,1,0:T(8,128)(2,1)}), bf16[3,768,384]{2,1,0:T(8,128)(2,1)}) %all-gather.14.cloned.1.call-update) | async-done | bytes 1769488 | tf_op jit(solution)/shard_map/all_gather | solution.py:213
  99.0 3.5 convolution_bitcast_fusion.1
  107.6 3.3 copy.110
  113.3 4.2 fusion.101
  117.6 33.9 %while.40 = (s32[]{:T(128)}, bf16[6,1,1024,64]{2,3,1,0:T(8,128)(2,1)S(1)}, bf16[6,1,1024,64]{3,2,1,0:T(8,128)(2,1)}, bf16[6,1,1024,64]{3,2,1,0:T(8,128)(2,1)}, b...) while((s32[]{:T(128)}, bf16[6,1,1024,64]{2,3,1,0:T(8,128)(2,1)S(1)}, ...), condition=%wide.region_14.15_spmd.clone, body=%wide.region_11.0_spmd.clone.sunk | while | flops 281082880 | bytes 13527121 | solution.py:129
  159.9 4.9 fusion.99
  165.7 35.2 %while.39 = (s32[]{:T(128)}, bf16[6,1,1024,64]{2,3,1,0:T(8,128)(2,1)}, f32[6,1,1024]{2,1,0:T(1,128)}, bf16[6,1,1024,64]{3,2,1,0:T(8,128)(2,1)S(1)}, bf16[6,1,102...) while((s32[]{:T(128)}, ...), condition=%wide.region_3.4_spmd.clone, body=%wide.region_0.3_spmd.clone.sunk | while | flops 281083904 | bytes 13548121 | solution.py:129
  200.9 5.0 fusion.177
  213.1 36.0 %reduce-scatter.10.cloned.1.call-done = f32[512,768]{1,0:T(8,128)} async-done(((f32[1024,768]{1,0:T(8,128)}), f32[512,768]{1,0:T(8,128)}) %reduce-scatter.10.cloned.1.call-update) | async-done | bytes 1572880 | tf_op jit(solution)/shard_map/reduce_scatter | solution.py:38
  253.7 39.9 %all-gather.28.cloned.1.call-done = bf16[768,1536]{1,0:T(8,128)(2,1)} async-done(((bf16[48,1536]{1,0:T(8,128)(2,1)}), bf16[768,1536]{1,0:T(8,128)(2,1)}) %all-gather.28.cloned.1.call-update) | async-done | bytes 2359312 | tf_op jit(solution)/shard_map/all_gather | solution.py:221
  293.6 43.3 %all-gather.30.cloned.1.call-done = bf16[1536,768]{0,1:T(8,128)(2,1)} async-done(((bf16[1536,48]{0,1:T(8,128)(2,1)}), bf16[1536,768]{0,1:T(8,128)(2,1)}) %all-gather.30.cloned.1.call-update) | async-done | bytes 2359312 | tf_op jit(solution)/shard_map/all_gather | solution.py:222
  336.8 27.6 %all-gather.26.cloned.1.call-done = bf16[1024,768]{1,0:T(8,128)(2,1)} async-done(((bf16[512,768]{1,0:T(8,128)(2,1)}), bf16[1024,768]{1,0:T(8,128)(2,1)}) %all-gather.26.cloned.1.call-update) | async-done | bytes 1572880 | tf_op jit(solution)/shard_map/all_gather | solution.py:47
  364.4 22.1 %fusion.98 = f32[1024,768]{1,0:T(8,128)} fusion(bf16[1536,768]{0,1:T(8,128)(2,1)} %all-gather.30.cloned.1.call-done, bf16[1024,768]{1,0:T(8,128)(2,1)} %all-gather.26.cloned.1.call-done, bf16[768,1536]{1,0:T(8,128)(2,1)} %all-gather.28.cloned.1.call-done, f32[1536]{0:T(1024)S(1)} %dynamic_slice.71), kind=kOutput, calls=%fused_computation.140 | convolution fusion | flops 4935647232 | bytes 9443328 | tf_op jit(solution)/shard_map/dot_general | solution.py:57
  387.3 22.3 %all-gather.18.cloned.1.call-done = bf16[768,1536]{1,0:T(8,128)(2,1)} async-done(((bf16[48,1536]{1,0:T(8,128)(2,1)}), bf16[768,1536]{1,0:T(8,128)(2,1)}) %all-gather.18.cloned.1.call-update) | async-done | bytes 2359312 | tf_op jit(solution)/shard_map/all_gather | solution.py:215
  409.6 28.2 %all-gather.16.cloned.1.call-done = bf16[1024,768]{1,0:T(8,128)(2,1)} async-done(((bf16[512,768]{1,0:T(8,128)(2,1)}), bf16[1024,768]{1,0:T(8,128)(2,1)}) %all-gather.16.cloned.1.call-update) | async-done | bytes 1572880 | tf_op jit(solution)/shard_map/all_gather | solution.py:47
  437.8 19.9 %multiply_convert_fusion.1 = (bf16[1024,1536]{1,0:T(8,128)(2,1)}, f32[1024,1536]{1,0:T(8,128)}, f32[1024,1536]{1,0:T(8,128)}) fusion(f32[1536]{0:T(1024)S(1)} %dynamic_slice.67, bf16[1024,768]{1,0:T(8,128)(2,1)} %all-gather.16.cloned.1.call-done, bf16[768,1536]{1,0:T(8,128)(2,1)} %all-gather.18.cloned.1.call-done), kind=kOutput, calls=%fused_computation.113 | convolution fusion | flops 2519728128 | bytes 19666944 | tf_op jit(solution)/shard_map/dot_general | solution.py:139
  457.7 25.1 %all-gather.20.cloned.1.call-done = bf16[1536,768]{0,1:T(8,128)(2,1)} async-done(((bf16[1536,48]{0,1:T(8,128)(2,1)}), bf16[1536,768]{0,1:T(8,128)(2,1)}) %all-gather.20.cloned.1.call-update) | async-done | bytes 2359312 | tf_op jit(solution)/shard_map/all_gather | solution.py:216
  482.8 6.9 fusion.178
  489.8 37.5 %reduce-scatter.16.cloned.1.call-done = f32[512,768]{1,0:T(8,128)} async-done(((f32[1024,768]{1,0:T(8,128)}), f32[512,768]{1,0:T(8,128)}) %reduce-scatter.16.cloned.1.call-update) | async-done | bytes 1572880 | tf_op jit(solution)/shard_map/reduce_scatter | solution.py:38
  531.6 41.2 %reduce-scatter.12.cloned.1.call-done = f32[512,768]{1,0:T(8,128)} async-done(((f32[1024,768]{1,0:T(8,128)}), f32[512,768]{1,0:T(8,128)}) %reduce-scatter.12.cloned.1.call-update) | async-done | bytes 1572880 | tf_op jit(solution)/shard_map/reduce_scatter | solution.py:38
  577.9 3.3 bitcast_convert_fusion
  581.2 38.1 %all-gather.32.cloned.1.call-done = f32[1024,768]{1,0:T(8,128)} async-done(((f32[512,768]{1,0:T(8,128)}), f32[1024,768]{1,0:T(8,128)}) %all-gather.32.cloned.1.call-update) | async-done | bytes 3145744 | tf_op jit(solution)/shard_map/all_gather | solution.py:51
  619.3 3.0 gather_fusion.1
  622.3 43.4 %all-gather.22.cloned.1.call-done = f32[1024,768]{1,0:T(8,128)} async-done(((f32[512,768]{1,0:T(8,128)}), f32[1024,768]{1,0:T(8,128)}) %all-gather.22.cloned.1.call-update) | async-done | bytes 3145744 | tf_op jit(solution)/shard_map/all_gather | solution.py:51
  665.7 3.7 gather_fusion
  671.2 5.5 scatter_custom_fusion
  682.1 27.3 %all-gather.34.cloned.1.call-done = bf16[1024,768]{1,0:T(8,128)(2,1)} async-done(((bf16[512,768]{1,0:T(8,128)(2,1)}), bf16[1024,768]{1,0:T(8,128)(2,1)}) %all-gather.34.cloned.1.call-update) | async-done | bytes 1572880 | tf_op jit(solution)/shard_map/all_gather | solution.py:47
  709.4 10.3 convert_reduce_fusion
  721.4 4.3 fusion.180
  725.8 43.5 %reduce-scatter.18.cloned.1.call-done = f32[512,768]{1,0:T(8,128)} async-done(((f32[1024,768]{1,0:T(8,128)}), f32[512,768]{1,0:T(8,128)}) %reduce-scatter.18.cloned.1.call-update) | async-done | bytes 1572880 | tf_op jit(solution)/shard_map/reduce_scatter | solution.py:38
  774.4 6.1 fusion.182
  782.1 6.4 fusion.183
  788.5 12.6 %all-gather.36.cloned.1.call-done = bf16[1024,768]{1,0:T(8,128)(2,1)} async-done(((bf16[512,768]{1,0:T(8,128)(2,1)}), bf16[1024,768]{1,0:T(8,128)(2,1)}) %all-gather.36.cloned.1.call-update) | async-done | bytes 1572880 | tf_op jit(solution)/shard_map/all_gather | solution.py:47
  806.1 79.7 %while.41 = (s32[]{:T(128)}, bf16[6,1,1024,64]{2,3,1,0:T(8,128)(2,1)S(1)}, bf16[6,1,1024,64]{2,3,1,0:T(8,128)(2,1)}, bf16[6,1,1024,64]{2,3,1,0:T(8,128)(2,1)S(1)...) while((s32[]{:T(128)}, ...), condition=%wide.region_31.32_spmd.clone, body=%wide.region_29.31_spmd.clone.sunk | while | flops 687144960 | bytes 33723508 | solution.py:286
  890.5 6.2 convolution_bitcast_fusion.2
  896.7 6.4 copy.119
  903.1 3.8 fusion.181
  907.2 6.1 convolution_bitcast_fusion.3
  920.2 39.3 %reduce-scatter.26.cloned.1.call-done = f32[1536,48]{0,1:T(8,128)} async-done(((f32[1536,768]{0,1:T(8,128)}), f32[1536,48]{0,1:T(8,128)}) %reduce-scatter.26.cloned.1.call-update) | async-done | bytes 294928 | tf_op jit(solution)/shard_map/reduce_scatter | solution.py:302
  975.9 103.6 %all-reduce.4.cloned.1.call-done = f32[3,768,384]{2,0,1:T(4,128)} async-done(((f32[3,768,384]{2,0,1:T(4,128)}), f32[3,768,384]{2,0,1:T(4,128)}) %all-reduce.4.cloned.1.call-update) | async-done | bytes 3538960
  1080.5 61.4 %reduce-scatter.22.cloned.1.call-done = f32[384,48]{0,1:T(8,128)} async-done(((f32[384,768]{0,1:T(8,128)}), f32[384,48]{0,1:T(8,128)}) %reduce-scatter.22.cloned.1.call-update) | async-done | bytes 73744 | tf_op jit(solution)/shard_map/reduce_scatter | solution.py:300
  1145.0 42.3 %reduce-scatter.20.cloned.1.call-done = f32[512,768]{1,0:T(8,128)} async-done(((f32[1024,768]{1,0:T(8,128)}), f32[512,768]{1,0:T(8,128)}) %reduce-scatter.20.cloned.1.call-update) | async-done | bytes 1572880 | tf_op jit(solution)/shard_map/reduce_scatter | solution.py:38
  1194.2 3.3 convert_bitcast_fusion
  1197.5 40.1 %all-reduce.1 = (f32[6]{0:T(128)S(1)}, f32[6]{0:T(128)S(1)}, f32[9216]{0:T(1024)S(1)}) all-reduce(f32[6]{0:T(128)S(1)} %pad_maximum_fusion.5, f32[6]{0:T(128)S(1)} %pad_maximum_fusion.4, f32[9216]{0:T(1024)S(1)} %copy-done.35), channel_id=1, replica_groups=mesh['dp'=16,'mp'=2] {'dp','mp'}, use_global_device_ids=true, to_apply=%region_46.47 | all-reduce | flops 9228 | bytes 73824 | tf_op jit(solution)/shard_map/psum | solution.py:341
  1244.7 3.8 copy.176
  (389 shorter events, 260.5 us)
Async XLA Ops:
  7.2 55.6 %all-gather.24.cloned.1.call-start = ((), (), s32[]{:S(2)}) async-start(), calls=%async_computation.16 | async-start | bytes 1880064 | tf_op jit(solution)/shard_map/all_gather | solution.py:219
  7.9 91.1 %all-gather.14.cloned.1.call-start = ((), (), s32[]{:S(2)}) async-start(), calls=%async_computation.9 | async-start | bytes 1880064 | tf_op jit(solution)/shard_map/all_gather | solution.py:213
  9.6 197.6 %reduce-scatter.14.cloned.1.call-start = ((), (), s32[]{:S(2)}) async-start(), calls=%async_computation.17 | async-start | bytes 4718592 | tf_op jit(solution)/shard_map/reduce_scatter | solution.py:38
  67.8 31.2 %copy-start.27 = (bf16[1,1024,768]{2,1,0:T(8,128)(2,1)S(1)}, bf16[1,1024,768]{2,1,0:T(8,128)(2,1)}, u32[]{:S(2)}) copy-start(bf16[1,1024,768]{2,1,0:T(8,128)(2,1)} %param.31) | copy-start | bytes 4718596
  117.6 33.9 %copy-start.16 = (bf16[384,768]{0,1:T(8,128)(2,1)S(1)}, bf16[384,768]{0,1:T(8,128)(2,1)}, u32[]{:S(2)}) copy-start(bf16[384,768]{0,1:T(8,128)(2,1)} %all_gather.52) | copy-start | bytes 1769476
  154.3 94.8 %reduce-scatter.10.cloned.1.call-start = ((), (), s32[]{:S(2)}) async-start(), calls=%async_computation.10 | async-start | bytes 4718592 | tf_op jit(solution)/shard_map/reduce_scatter | solution.py:38
  205.9 87.6 %all-gather.28.cloned.1.call-start = ((), (), s32[]{:S(2)}) async-start(), calls=%async_computation.19 | async-start | bytes 2506752 | tf_op jit(solution)/shard_map/all_gather | solution.py:221
  206.5 130.3 %all-gather.30.cloned.1.call-start = ((), (), s32[]{:S(2)}) async-start(), calls=%async_computation.20 | async-start | bytes 2506752 | tf_op jit(solution)/shard_map/all_gather | solution.py:222
  207.1 157.3 %all-gather.26.cloned.1.call-start = ((), (), s32[]{:S(2)}) async-start(), calls=%async_computation.18 | async-start | bytes 2359296 | tf_op jit(solution)/shard_map/all_gather | solution.py:47
  212.3 197.3 %all-gather.18.cloned.1.call-start = ((), (), s32[]{:S(2)}) async-start(), calls=%async_computation.12 | async-start | bytes 2506752 | tf_op jit(solution)/shard_map/all_gather | solution.py:215
  213.0 224.7 %all-gather.16.cloned.1.call-start = ((), (), s32[]{:S(2)}) async-start(), calls=%async_computation.11 | async-start | bytes 2359296 | tf_op jit(solution)/shard_map/all_gather | solution.py:47
  252.5 230.3 %all-gather.20.cloned.1.call-start = ((), (), s32[]{:S(2)}) async-start(), calls=%async_computation.13 | async-start | bytes 2506752 | tf_op jit(solution)/shard_map/all_gather | solution.py:216
  253.3 273.9 %reduce-scatter.16.cloned.1.call-start = ((), (), s32[]{:S(2)}) async-start(), calls=%async_computation.21 | async-start | bytes 4718592 | tf_op jit(solution)/shard_map/reduce_scatter | solution.py:38
  386.6 186.2 %reduce-scatter.12.cloned.1.call-start = ((), (), s32[]{:S(2)}) async-start(), calls=%async_computation.14 | async-start | bytes 4718592 | tf_op jit(solution)/shard_map/reduce_scatter | solution.py:38
  387.3 70.3 %copy-start.52 = (f32[1536]{0:T(1024)}, f32[1536]{0:T(1024)S(1)}, u32[]{:S(2)}) copy-start(f32[1536]{0:T(1024)S(1)} %dynamic_slice.67) | copy-start | bytes 18436
  489.7 37.5 %copy-start.47 = (f32[768]{0:T(1024)S(1)}, f32[768]{0:T(1024)}, u32[]{:S(2)}) copy-start(f32[768]{0:T(1024)} %get-tuple-element.373) | copy-start | bytes 9220
  489.7 129.6 %all-gather.32.cloned.1.call-start = ((), (), s32[]{:S(2)}) async-start(), calls=%async_computation.22 | async-start | bytes 4718592 | tf_op jit(solution)/shard_map/all_gather | solution.py:51
  529.6 43.2 %copy-start.48 = (f32[768]{0:T(1024)S(1)}, f32[768]{0:T(1024)}, u32[]{:S(2)}) copy-start(f32[768]{0:T(1024)} %get-tuple-element.364) | copy-start | bytes 9220
  531.4 134.3 %all-gather.22.cloned.1.call-start = ((), (), s32[]{:S(2)}) async-start(), calls=%async_computation.15 | async-start | bytes 4718592 | tf_op jit(solution)/shard_map/all_gather | solution.py:51
  576.7 132.7 %all-gather.34.cloned.1.call-start = ((), (), s32[]{:S(2)}) async-start(), calls=%async_computation.23 | async-start | bytes 2359296 | tf_op jit(solution)/shard_map/all_gather | solution.py:47
  679.1 30.3 %copy-start.53 = (f32[1536]{0:T(1024)S(1)}, f32[1536]{0:T(1024)}, u32[]{:S(2)}) copy-start(f32[1536]{0:T(1024)} %copy-done.52) | copy-start | bytes 18436
  682.0 87.2 %reduce-scatter.18.cloned.1.call-start = ((), (), s32[]{:S(2)}) async-start(), calls=%async_computation.24 | async-start | bytes 4718592 | tf_op jit(solution)/shard_map/reduce_scatter | solution.py:38
  725.7 43.6 %copy-start.4 = (f32[512,768]{1,0:T(8,128)S(1)}, f32[512,768]{1,0:T(8,128)}, u32[]{:S(2)}) copy-start(f32[512,768]{1,0:T(8,128)} %copy-done.3) | copy-start | bytes 4718596
  725.7 46.4 %copy-start.41 = (f32[512]{0:T(512)S(1)}, f32[512]{0:T(512)}, u32[]{:S(2)}) copy-start(f32[512]{0:T(512)} %copy-done.40) | copy-start | bytes 6148
  725.7 75.4 %all-gather.36.cloned.1.call-start = ((), (), s32[]{:S(2)}) async-start(), calls=%async_computation.25 | async-start | bytes 2359296 | tf_op jit(solution)/shard_map/all_gather | solution.py:47
  773.8 143.6 %reduce-scatter.24.cloned.1.call-start = ((), (), s32[]{:S(2)}) async-start(), calls=%async_computation.29 | async-start | bytes 5013504 | tf_op jit(solution)/shard_map/reduce_scatter | solution.py:301
  780.5 179.0 %reduce-scatter.26.cloned.1.call-start = ((), (), s32[]{:S(2)}) async-start(), calls=%async_computation.30 | async-start | bytes 5013504 | tf_op jit(solution)/shard_map/reduce_scatter | solution.py:302
  788.5 291.1 %all-reduce.4.cloned.1.call-start = ((), (), s32[]{:S(2)}) async-start(), calls=%async_computation.31 | async-start | bytes 9437184
  903.1 238.8 %reduce-scatter.22.cloned.1.call-start = ((), (), s32[]{:S(2)}) async-start(), calls=%async_computation.28 | async-start | bytes 1253376 | tf_op jit(solution)/shard_map/reduce_scatter | solution.py:300
  906.9 280.3 %reduce-scatter.20.cloned.1.call-start = ((), (), s32[]{:S(2)}) async-start(), calls=%async_computation.26 | async-start | bytes 4718592 | tf_op jit(solution)/shard_map/reduce_scatter | solution.py:38
  913.4 46.1 %copy-start.12 = (f32[1536,48]{0,1:T(8,128)S(1)}, f32[1536,48]{0,1:T(8,128)}, u32[]{:S(2)}) copy-start(f32[1536,48]{0,1:T(8,128)} %param.39) | copy-start | bytes 884740
  913.4 331.4 %all-gather.38.cloned.1.call-start = ((), (), s32[]{:S(2)}) async-start(), calls=%async_computation.27 | async-start | bytes 4718592 | tf_op jit(solution)/shard_map/all_gather | solution.py:51
  917.3 51.5 %copy-start.50 = (f32[768]{0:T(1024)S(1)}, f32[768]{0:T(1024)}, u32[]{:S(2)}) copy-start(f32[768]{0:T(1024)} %get-tuple-element.263) | copy-start | bytes 9220
  917.3 52.8 %copy-start.49 = (f32[768]{0:T(1024)S(1)}, f32[768]{0:T(1024)}, u32[]{:S(2)}) copy-start(f32[768]{0:T(1024)} %get-tuple-element.266) | copy-start | bytes 9220
  920.2 221.7 %copy-start.26 = (f32[384,48]{0,1:T(8,128)S(1)}, f32[384,48]{0,1:T(8,128)}, u32[]{:S(2)}) copy-start(f32[384,48]{0,1:T(8,128)} %param.37) | copy-start | bytes 221188
  962.5 181.1 %copy-start.17 = (f32[3,48,384]{2,1,0:T(8,128)S(1)}, f32[3,48,384]{2,1,0:T(8,128)}, u32[]{:S(2)}) copy-start(f32[3,48,384]{2,1,0:T(8,128)} %param.36) | copy-start | bytes 663556
  1143.6 97.2 %copy-start.28 = (f32[384,48]{0,1:T(8,128)}, f32[384,48]{0,1:T(8,128)S(1)}, u32[]{:S(2)}) copy-start(f32[384,48]{0,1:T(8,128)S(1)} %get-tuple-element.649) | copy-start | bytes 221188
  1143.6 97.2 %copy-start.29 = (f32[384,48]{0,1:T(8,128)}, f32[384,48]{0,1:T(8,128)S(1)}, u32[]{:S(2)}) copy-start(f32[384,48]{0,1:T(8,128)S(1)} %get-tuple-element.653) | copy-start | bytes 221188
  1145.0 96.5 %copy-start.24 = (f32[3,48,384]{2,1,0:T(8,128)}, f32[3,48,384]{2,1,0:T(8,128)S(1)}, u32[]{:S(2)}) copy-start(f32[3,48,384]{2,1,0:T(8,128)S(1)} %get-tuple-element.648) | copy-start | bytes 663556
  1145.0 96.5 %copy-start.25 = (f32[3,48,384]{2,1,0:T(8,128)}, f32[3,48,384]{2,1,0:T(8,128)S(1)}, u32[]{:S(2)}) copy-start(f32[3,48,384]{2,1,0:T(8,128)S(1)} %get-tuple-element.652) | copy-start | bytes 663556
  1190.0 52.3 %copy-start.30 = (f32[9216]{0:T(1024)S(1)}, f32[9216]{0:T(1024)}, u32[]{:S(2)}) copy-start(f32[9216]{0:T(1024)} %param.48) | copy-start | bytes 110596
  1190.0 52.3 %copy-start.36 = (f32[9216]{0:T(1024)S(1)}, f32[9216]{0:T(1024)}, u32[]{:S(2)}) copy-start(f32[9216]{0:T(1024)} %param.50) | copy-start | bytes 110596
  1190.0 52.3 %copy-start.37 = (f32[9216]{0:T(1024)S(1)}, f32[9216]{0:T(1024)}, u32[]{:S(2)}) copy-start(f32[9216]{0:T(1024)} %param.49) | copy-start | bytes 110596
  1190.1 52.9 %copy-start.22 = (f32[1536,48]{0,1:T(8,128)S(1)}, f32[1536,48]{0,1:T(8,128)}, u32[]{:S(2)}) copy-start(f32[1536,48]{0,1:T(8,128)} %get-tuple-element.651) | copy-start | bytes 884740
  1190.1 52.9 %copy-start.23 = (f32[1536,48]{0,1:T(8,128)S(1)}, f32[1536,48]{0,1:T(8,128)}, u32[]{:S(2)}) copy-start(f32[1536,48]{0,1:T(8,128)} %get-tuple-element.655) | copy-start | bytes 884740
  1194.2 49.7 %copy-start.14 = (f32[48,1536]{1,0:T(8,128)S(1)}, f32[48,1536]{1,0:T(8,128)}, u32[]{:S(2)}) copy-start(f32[48,1536]{1,0:T(8,128)} %param.38) | copy-start | bytes 884740
  1194.2 49.7 %copy-start.20 = (f32[48,1536]{1,0:T(8,128)S(1)}, f32[48,1536]{1,0:T(8,128)}, u32[]{:S(2)}) copy-start(f32[48,1536]{1,0:T(8,128)} %get-tuple-element.650) | copy-start | bytes 884740
  1194.2 49.7 %copy-start.21 = (f32[48,1536]{1,0:T(8,128)S(1)}, f32[48,1536]{1,0:T(8,128)}, u32[]{:S(2)}) copy-start(f32[48,1536]{1,0:T(8,128)} %get-tuple-element.654) | copy-start | bytes 884740
  (34 other events, 123.2 us)
Sparse Core Ops, SparseCore 0:
  10.3 46.7 all-gather.23
  60.1 38.8 all-gather.13
  154.4 42.2 reduce-scatter.13
  206.0 42.9 reduce-scatter.9
  251.2 42.3 all-gather.27
  295.7 41.0 all-gather.29
  338.4 25.9 all-gather.25
  367.3 42.3 all-gather.17
  411.7 25.9 all-gather.15
  440.5 42.3 all-gather.19
  485.1 42.1 reduce-scatter.15
  529.4 43.3 reduce-scatter.11
  574.4 44.9 all-gather.31
  620.7 44.9 all-gather.21
  682.1 27.2 all-gather.33
  725.8 43.3 reduce-scatter.17
  773.9 27.2 all-gather.35
  805.3 75.5 reduce-scatter.23
  884.8 74.6 reduce-scatter.25
  963.4 116.0 all-reduce.3
  1084.1 57.7 reduce-scatter.21
  1144.8 42.3 reduce-scatter.19
  1190.1 46.1 all-gather.37
where the time goes:
time: 1270 us; the launch traced here: 1260 us
  waiting for transfers between devices  744 us (59%)
  matrix products  217 us (17%)
  other arithmetic  111 us (9%)
  blocking collectives  88.9 us (7%)
  local copies, waits for them, and re-layouts  73.5 us (6%)
  between operations  17.8 us (1%)
    reduce_scatter x6, waiting for transfers between devices, row_share(): lax.psum_scatter(term_fn(jnp.int32(0), share_rows * lax.axis_size('mp')),...  200 us
    unnamed x24, waiting for transfers between devices  106 us
    all_gather x4, waiting for transfers between devices, row_join_low(): return lax.all_gather(share_values, 'mp', axis=0, tiled=True)  95.7 us
    all_gather x3, waiting for transfers between devices, row_join(): return lax.all_gather(share_values, 'mp', axis=0, tiled=True)  81.5 us
    reduce_scatter x1, waiting for transfers between devices, local(): lax.psum_scatter(grad_out, 'dp', scatter_dimension=1, tiled=True)  61.4 us
    all_gather x1, waiting for transfers between devices, local(): lax.all_gather(teacher_down, 'dp', axis=1, tiled=True)  43.3 us
    dot_general x5, matrix products, term_fn(): return jnp.dot(left_rows, right_matrix, preferred_element_type=jnp.float32)  40.9 us
    psum x1, blocking collectives, local(): lax.psum((matrix_squares(attn_weight, out_weight, up_weight, down_weight)...  40.1 us
  transfers between devices with their start and end apart: 23, of which 19 were waited for; matrix products, arithmetic and copies ran while one was open for 24% of the time, Pallas kernels for 0%

commit v1 on v0

--- a/solution.py
+++ b/solution.py
@@ -176,7 +176,7 @@
     )
 
 
-def local(
+def split_units(
     tokens,
     teacher_tokens,
     cotangent,
@@ -380,9 +380,289 @@
     )
 
 
+def shard_pack(attn_w, out_w, up_w, down_w):
+    return jnp.concatenate(
+        [attn_w[0], attn_w[1], attn_w[2], out_w.T, up_w, down_w.T], axis=1
+    )
+
+
+def vector_pieces(packed, model_width):
+    return vector_parts(packed, model_width)
+
+
+def cosine_pull(rows, places, aimed, row_start):
+    row_count = rows.shape[0]
+    local_at = places - row_start
+    here = (local_at >= 0) & (local_at < row_count)
+    picked = rows[jnp.clip(local_at, 0, row_count - 1)]
+    inner = jnp.sum(picked * aimed, -1, keepdims=True)
+    square_own = jnp.sum(picked * picked, -1, keepdims=True) + cosine_eps
+    square_aim = jnp.sum(aimed * aimed, -1, keepdims=True) + cosine_eps
+    inverse = lax.rsqrt(square_own) * lax.rsqrt(square_aim)
+    pull = -cosine_weight * (aimed * inverse - picked * (inner * inverse / square_own))
+    pull = jnp.where(here[:, None], pull, 0.0)
+    return jnp.zeros_like(rows).at[jnp.clip(local_at, 0, row_count - 1)].add(pull)
+
+
+def heads_of(flat):
+    return flat.reshape(flat.shape[0], flat.shape[1] // HDIM, HDIM).transpose(1, 0, 2)
+
+
+def flat_of(split):
+    return split.transpose(1, 0, 2).reshape(split.shape[1], -1)
+
+
+def dot32(left, right):
+    return jnp.dot(left, right, preferred_element_type=jnp.float32)
+
+
+def dot_nt(left, right):
+    return lax.dot_general(
+        left, right, (((1,), (1,)), ((), ())), preferred_element_type=jnp.float32
+    )
+
+
+def dot_tn(left, right):
+    return lax.dot_general(
+        left, right, (((0,), (0,)), ((), ())), preferred_element_type=jnp.float32
+    )
+
+
+def split_rows(
+    tokens,
+    teacher_tokens,
+    cotangent,
+    lengths,
+    masked,
+    attn_weight,
+    out_weight,
+    up_weight,
+    down_weight,
+    attn_first,
+    out_first,
+    up_first,
+    down_first,
+    attn_second,
+    out_second,
+    up_second,
+    down_second,
+    vectors,
+    vector_first,
+    vector_second,
+    teacher_attn,
+    teacher_out,
+    teacher_up,
+    teacher_down,
+    teacher_vectors,
+):
+    low = jnp.bfloat16
+    everyone = ("dp", "mp")
+    shard_at = lax.axis_index("mp")
+    halves = lax.axis_size("mp")
+    seq_count, length, width = tokens.shape
+    rows = length // halves
+    row_start = shard_at * rows
+    part = attn_weight.shape[2]
+    units = up_weight.shape[1]
+    cuts = [0, part, 2 * part, 3 * part, 4 * part, 4 * part + units, 4 * part + 2 * units]
+    visible = (jnp.arange(length) < lengths[0])[None, None, :]
+    places = masked[0]
+
+    student = lax.all_gather(
+        shard_pack(attn_weight, out_weight, up_weight, down_weight).astype(low),
+        ("mp", "dp"),
+        axis=0,
+        tiled=True,
+    ).reshape(halves, width, cuts[6])
+    teacher = lax.all_gather(
+        shard_pack(teacher_attn, teacher_out, teacher_up, teacher_down),
+        "dp",
+        axis=0,
+        tiled=True,
+    )
+
+    def whole(index):
+        return jnp.concatenate(
+            [student[half, :, cuts[index] : cuts[index + 1]] for half in range(halves)], axis=1
+        )
+
+    teacher_parts = vector_parts(teacher_vectors.astype(jnp.float32), width)
+    bias_q = lax.dynamic_slice_in_dim(teacher_parts[0], shard_at * part, part)
+    bias_v = lax.dynamic_slice_in_dim(teacher_parts[1], shard_at * part, part)
+    bias_up = lax.dynamic_slice_in_dim(teacher_parts[8], shard_at * units, units)
+    teacher_rows = teacher_tokens[0]
+    listed = teacher_rows[places]
+    t_query = (dot32(listed, teacher[:, : cuts[1]]) + bias_q).astype(low)
+    t_keys = dot32(teacher_rows, teacher[:, cuts[1] : cuts[2]]).astype(low)
+    t_values = (dot32(teacher_rows, teacher[:, cuts[2] : cuts[3]]) + bias_v).astype(low)
+    t_mixed, unused_log = head_forward(
+        heads_of(t_query), heads_of(t_keys), heads_of(t_values), visible[0]
+    )
+    t_branch = lax.psum(dot_nt(flat_of(t_mixed), teacher[:, cuts[3] : cuts[4]]), "mp")
+    t_first = listed.astype(jnp.float32) + t_branch + teacher_parts[2]
+    t_normed = layer_norm(t_first, teacher_parts[3], teacher_parts[4])
+    t_gate = dot32(t_normed.astype(low), teacher[:, cuts[4] : cuts[5]]) + bias_up
+    t_act = jax.nn.gelu(t_gate, approximate=False).astype(low)
+    t_feed = lax.psum(dot_nt(t_act, teacher[:, cuts[5] : cuts[6]]), "mp")
+    aimed = layer_norm(t_normed + t_feed + teacher_parts[5], teacher_parts[6], teacher_parts[7])
+
+    pieces = vector_parts(vectors, width)
+    all_rows = tokens[0]
+    own_rows = lax.dynamic_slice_in_dim(all_rows, row_start, rows, 0)
+    w_q, w_k, w_v, w_out, w_up, w_down = [whole(index) for index in range(6)]
+    query = heads_of((dot32(own_rows, w_q) + pieces[0]).astype(low))
+    keys = heads_of(dot32(all_rows, w_k).astype(low))
+    values = heads_of((dot32(all_rows, w_v) + pieces[1]).astype(low))
+    mixed, log_total = lax.map(
+        lambda g: jax.tree.map(
+            lambda v: v[0], head_forward(g[0][None], g[1][None], g[2][None], visible[0])
+        ),
+        (query, keys, values),
+    )
+    attended = flat_of(mixed)
+    first_sum = own_rows.astype(jnp.float32) + dot_nt(attended, w_out) + pieces[2]
+    normed = layer_norm(first_sum, pieces[3], pieces[4])
+    normed_low = normed.astype(low)
+    gate_in = dot32(normed_low, w_up) + pieces[8]
+    activated = jax.nn.gelu(gate_in, approximate=False).astype(low)
+    second_sum = normed + dot_nt(activated, w_down) + pieces[5]
+    outcome = layer_norm(second_sum, pieces[6], pieces[7])
+    student_out = lax.all_gather(outcome.astype(low), "mp", axis=0, tiled=True)[None]
+
+    own_cotangent = lax.dynamic_slice_in_dim(cotangent[0], row_start, rows, 0)
+    grad_top = own_cotangent.astype(jnp.float32) + cosine_pull(outcome, places, aimed, row_start)
+    unused_top, pull_top = jax.vjp(layer_norm, second_sum, pieces[6], pieces[7])
+    grad_second, grad_gain_two, grad_shift_two = pull_top(grad_top)
+    feed_low = grad_second.astype(low)
+    grad_down = dot_tn(feed_low, activated)
+    grad_act = dot32(feed_low, w_down)
+    unused_gelu, pull_gelu = jax.vjp(partial(jax.nn.gelu, approximate=False), gate_in)
+    (grad_gate,) = pull_gelu(grad_act)
+    gate_low = grad_gate.astype(low)
+    grad_up = dot_tn(normed_low, gate_low)
+    grad_normed = grad_second + dot_nt(gate_low, w_up)
+    unused_mid, pull_mid = jax.vjp(layer_norm, first_sum, pieces[3], pieces[4])
+    grad_first, grad_gain_one, grad_shift_one = pull_mid(grad_normed)
+    branch_low = grad_first.astype(low)
+    grad_out = dot_tn(branch_low, attended)
+    grad_heads = heads_of(dot32(branch_low, w_out).astype(low))
+
+    def one_head(g):
+        query_h, keys_h, values_h, mixed_h, log_h = g
+        scale_factor = HDIM**-0.5
+        scores = jnp.where(visible[0], dot_nt(query_h, keys_h) * scale_factor, masked_score)
+        probs = jnp.exp(scores - log_h[:, None])
+        grad_probs = dot_nt(mixed_h, values_h)
+        inner = jnp.sum(probs * grad_probs, -1, keepdims=True)
+        grad_scores = (probs * (grad_probs - inner)).astype(low)
+        return (
+            (dot32(grad_scores, keys_h) * scale_factor).astype(low),
+            (dot_tn(grad_scores, query_h) * scale_factor).astype(low),
+            dot_tn(probs.astype(low), mixed_h).astype(low),
+        )
+
+    grad_query, grad_keys, grad_values = lax.map(
+        one_head, (query, keys, values, grad_heads, log_total)
+    )
+    grad_query = flat_of(grad_query)
+
+    def row_sum(term):
+        other = lax.dynamic_slice_in_dim(term, (1 - shard_at) * rows, rows, 0)
+        mine = lax.dynamic_slice_in_dim(term, row_start, rows, 0)
+        came = lax.ppermute(other, "mp", [(0, 1), (1, 0)])
+        return (mine.astype(jnp.float32) + came.astype(jnp.float32)).astype(low)
+
+    grad_keys = row_sum(flat_of(grad_keys))
+    grad_values = row_sum(flat_of(grad_values))
+    grad_q = dot_tn(own_rows, grad_query)
+    grad_k = dot_tn(own_rows, grad_keys)
+    grad_v = dot_tn(own_rows, grad_values)
+    input_own = (
+        grad_first + dot_nt(grad_query, w_q) + dot_nt(grad_keys, w_k) + dot_nt(grad_values, w_v)
+    )
+    input_grad = lax.all_gather(input_own, "mp", axis=0, tiled=True)[None]
+
+    def half_of(matrix, half):
+        span = matrix.shape[1] // halves
+        return matrix[:, half * span : (half + 1) * span]
+
+    grads = [grad_q, grad_k, grad_v, grad_out, grad_up, grad_down]
+    packed_grad = jnp.concatenate(
+        [
+            jnp.concatenate([half_of(g, half) for g in grads], axis=1).astype(low)
+            for half in range(halves)
+        ],
+        axis=0,
+    )
+    summed = lax.psum_scatter(
+        packed_grad, ("mp", "dp"), scatter_dimension=0, tiled=True
+    ).astype(jnp.float32)
+    summed_attn = jnp.stack([summed[:, cuts[i] : cuts[i + 1]] for i in range(3)])
+    summed_out = summed[:, cuts[3] : cuts[4]].T
+    summed_up = summed[:, cuts[4] : cuts[5]]
+    summed_down = summed[:, cuts[5] : cuts[6]].T
+
+    vector_grad = jnp.concatenate(
+        [
+            jnp.sum(grad_query.astype(jnp.float32), 0),
+            jnp.sum(grad_values.astype(jnp.float32), 0),
+            jnp.sum(branch_low.astype(jnp.float32), 0),
+            grad_gain_one,
+            grad_shift_one,
+            jnp.sum(feed_low.astype(jnp.float32), 0),
+            grad_gain_two,
+            grad_shift_two,
+            jnp.sum(gate_low.astype(jnp.float32), 0),
+        ]
+    )
+    return (student_out, input_grad) + lamb_update(
+        (summed_attn, summed_out, summed_up, summed_down),
+        (attn_weight, out_weight, up_weight, down_weight),
+        (attn_first, out_first, up_first, down_first),
+        (attn_second, out_second, up_second, down_second),
+        vector_grad,
+        vectors,
+        vector_first,
+        vector_second,
+    )
+
+
+def lamb_update(grads, weights, firsts, seconds, vector_grad, vectors, vector_first, vector_second):
+    moments, squares, steps = [], [], []
+    for grad_now, weight, first_old, second_old in zip(grads, weights, firsts, seconds):
+        first_new, second_new, step_now = adam_moments(grad_now, first_old, second_old)
+        moments.append(first_new)
+        squares.append(second_new)
+        steps.append(step_now + decay_rate * weight)
+    weight_total, update_total, vector_total = lax.psum(
+        (matrix_squares(*weights), matrix_squares(*steps), vector_grad), ("dp", "mp")
+    )
+    weight_norms = jnp.sqrt(weight_total)
+    update_norms = jnp.sqrt(update_total)
+    trust_ratio = weight_norms / update_norms
+    ratios = [trust_ratio[0:3][:, None, None], trust_ratio[3], trust_ratio[4], trust_ratio[5]]
+    updated = [
+        weight - matrix_rate * ratio * step for weight, ratio, step in zip(weights, ratios, steps)
+    ]
+    vector_moment, vector_square, step_vector = adam_moments(
+        vector_total, vector_first, vector_second
+    )
+    vector_updated = vectors - vector_rate * step_vector
+    return (
+        *updated,
+        *moments,
+        *squares,
+        vector_moment,
+        vector_square,
+        vector_updated,
+        jnp.stack([weight_norms, update_norms]),
+        trust_ratio,
+    )
+
+
 def solution(mesh):
     return jax.shard_map(
-        local,
+        split_rows,
         mesh=mesh,
         in_specs=(
             P("dp", None, None),

time: 1270 us -> 840 us (0.66)
  waiting for transfers between devices: 744 us -> 367 us
  blocking collectives: 88.9 us -> 40.7 us
  other arithmetic: 111 us -> 75.8 us
  local copies, waits for them, and re-layouts: 73.5 us -> 108 us
    all_gather x13 -> x4, waiting for transfers between devices: 337 us -> 143 us  [the longest x1 78.9 us: split_rows(): lax.all_gather(shard_pack(attn_weight, out_weight, up_weight, down_weight...]
    reduce_scatter x9 -> x1, waiting for transfers between devices: 301 us -> 154 us  [split_rows(): lax.psum_scatter(packed_grad, ('mp', 'dp'), scatter_dimension=0, tiled=True)]
    unnamed x24 -> x7, waiting for transfers between devices: 106 us -> 0.12 us
    all_gather x2 -> x0, blocking collectives: 48.8 us -> none  [the longest x1 27 us: local(): lax.all_gather(teacher_out, 'dp', axis=1, tiled=True)]
    psum x0 -> x2, waiting for transfers between devices: none -> 45 us  [the longest x1 24.3 us: split_rows(): lax.psum(dot_nt(flat_of(t_mixed), teacher[:, cuts[3]:cuts[4]]), 'mp')]
    ppermute x0 -> x2, waiting for transfers between devices: none -> 24.6 us  [row_sum(): came = lax.ppermute(other, 'mp', [(0, 1), (1, 0)])]
    slice x5 -> x13, local copies, waits for them, and re-layouts: 6.45 us -> 21.3 us  [the longest x12 20.7 us: half_of(): return matrix[:, half * span:(half + 1) * span]]
    convert_element_type x15, other arithmetic: 21.2 us -> 8.33 us  [the longest x12 3.03 us: one_head(): grad_scores = (probs * (grad_probs - inner)).astype(low)]
  transfers between devices with their start and end apart: 23 -> 9, of which waited for: 19 -> 6; matrix products, arithmetic and copies ran while one was open for 24% -> 11% of each run, Pallas kernels for 0% -> 0%
where the time goes in v1:
time: 840 us; the launch traced here: 829 us
  waiting for transfers between devices  367 us (44%)
  matrix products  214 us (25%)
  local copies, waits for them, and re-layouts  108 us (13%)
  other arithmetic  75.8 us (9%)
  blocking collectives  40.7 us (5%)
  between operations  19.3 us (2%)
    reduce_scatter x1, waiting for transfers between devices, split_rows(): lax.psum_scatter(packed_grad, ('mp', 'dp'), scatter_dimension=0, tiled=True)  154 us
    all_gather x1, waiting for transfers between devices, split_rows(): lax.all_gather(shard_pack(attn_weight, out_weight, up_weight, down_weight...  78.9 us
    all_gather x1, waiting for transfers between devices, split_rows(): lax.all_gather(shard_pack(teacher_attn, teacher_out, teacher_up, teacher_...  64.5 us
    dot_general x32, matrix products, dot_nt(): lax.dot_general(left, right, (((1,), (1,)), ((), ())), preferred_element_...  62.2 us
    dot_general x21, matrix products, dot32(): return jnp.dot(left, right, preferred_element_type=jnp.float32)  58.4 us
    dot_general x30, matrix products, dot_tn(): lax.dot_general(left, right, (((0,), (0,)), ((), ())), preferred_element_...  51.9 us
    psum x1, blocking collectives, lamb_update(): lax.psum((matrix_squares(*weights), matrix_squares(*steps), vector_grad),...  40.7 us
    unnamed x213, local copies, waits for them, and re-layouts  28.7 us
  transfers between devices with their start and end apart: 9, of which 6 were waited for; matrix products, arithmetic and copies ran while one was open for 11% of the time, Pallas kernels for 0%

profile of v1, /device:TPU:0, one launch (start us, length us, event | category | flops | bytes accessed | tf_op | source)
XLA Modules:
  0.0 829.3 jit_solution(6435410523350122760)
XLA Ops:
  19.0 64.5 %all-gather.9.cloned.1.call-done = bf16[768,4608]{1,0:T(8,128)(2,1)} async-done(((bf16[48,4608]{1,0:T(8,128)(2,1)}), bf16[768,4608]{1,0:T(8,128)(2,1)}) %all-gather.9.cloned.1.call-update) | async-done | bytes 7077904 | tf_op jit(solution)/shard_map/all_gather | solution.py:477
  86.8 2.8 fusion.245
  89.6 2.0 add_convert_fusion.4
  92.4 2.1 fusion.94
  94.7 24.3 %all-reduce.4.cloned.1.call-done = f32[128,768]{1,0:T(8,128)} async-done(((f32[128,768]{1,0:T(8,128)}), f32[128,768]{1,0:T(8,128)}) %all-reduce.4.cloned.1.call-update) | async-done | bytes 393232 | tf_op jit(solution)/shard_map/psum | solution.py:501
  121.3 6.1 fusion.61
  129.6 2.5 bitcast_convert_fusion
  132.6 20.8 %all-reduce.6.cloned.1.call-done = f32[128,768]{1,0:T(8,128)} async-done(((f32[128,768]{1,0:T(8,128)}), f32[128,768]{1,0:T(8,128)}) %all-reduce.6.cloned.1.call-update) | async-done | bytes 393232 | tf_op jit(solution)/shard_map/psum | solution.py:506
  155.3 78.9 %all-gather.5.cloned.1.call-done = bf16[1536,4608]{1,0:T(8,128)(2,1)} async-done(((bf16[48,4608]{1,0:T(8,128)(2,1)}), bf16[1536,4608]{1,0:T(8,128)(2,1)}) %all-gather.5.cloned.1.call-update) | async-done | bytes 14155792 | tf_op jit(solution)/shard_map/all_gather | solution.py:471
  234.2 4.0 slice_bitcast_fusion.5
  238.3 7.8 slice_bitcast_fusion.1
  248.7 4.0 add_convert_fusion.1
  252.8 4.2 copy.59
  256.9 2.8 convolution_convert_fusion.4
  259.8 2.7 copy.58
  262.6 69.7 %while.28 = (s32[]{:T(128)}, bf16[12,512,64]{1,2,0:T(8,128)(2,1)S(1)}, f32[12,512]{1,0:T(8,128)}, bf16[12,512,64]{2,1,0:T(8,128)(2,1)}, bf16[12,1024,64]{2,1,0:T...) while((s32[]{:T(128)}, ...), condition=%wide.region_3.4_spmd.clone, body=%wide.region_0.3_spmd.clone.sunk | while | flops 140542464 | bytes 7039077 | solution.py:516
  332.4 2.7 fusion.243
  335.6 19.5 %multiply_convert_fusion.1 = (bf16[512,3072]{1,0:T(8,128)(2,1)S(1)}, f32[512,3072]{1,0:T(8,128)}, f32[512,3072]{1,0:T(8,128)}) fusion(f32[3072]{0:T(1024)S(1)} %slice.225, bf16[768,1536]{1,0:T(8,128)(2,1)S(1)} %copy-done.11, bf16[768,1536]{1,0:T(8,128)(2,1)S(1)} %copy-done.13, f32[512,768]{1,0:T(8,128)S(1)} %get-tuple-element.312, ...), kind=kOutput, calls=%fused_computation.70 | convolution fusion | flops 2531131392 | bytes 22042624 | tf_op jit(solution)/shard_map/dot_general | solution.py:416
  355.1 2.8 fusion.244
  360.6 3.4 gather_fusion.1
  365.8 2.9 scatter_custom_fusion
  372.9 8.4 %convert_reduce_fusion = (f32[3072]{0:T(1024)S(1)}, bf16[512,3072]{1,0:T(8,128)(2,1)S(1)}) fusion(f32[512,3072]{1,0:T(8,128)} %get-tuple-element.253, bf16[512,768]{1,0:T(8,128)(2,1)S(1)} %get-tuple-element.231, bf16[768,1536]{1,0:T(8,128)(2,1)S(1)} %copy-done.18, bf16[768,1536]{1,0:T(8,128)(2,1)S(1)} %copy-done.16, f32[512,3072]{1,0:T(8,128)} %get-tuple-element.313, ...), kind=kOutput, calls=%fused_computation.68 | convolution fusion | flops 2452091904 | bytes 21258240 | tf_op jit(solution)/shard_map/dot_general | solution.py:416
  381.5 3.1 multiply_reduce_fusion.2
  384.6 4.9 convolution_convert_fusion.3
  394.8 110.2 %while.29 = (s32[]{:T(128)}, bf16[12,512,64]{1,2,0:T(8,128)(2,1)S(1)}, bf16[12,1024,64]{1,2,0:T(8,128)(2,1)}, bf16[12,1024,64]{1,2,0:T(8,128)(2,1)}, bf16[12,512...) while((s32[]{:T(128)}, ...), condition=%wide.region_26.27_spmd.clone, body=%wide.region_24.26_spmd.clone.sunk | while | flops 340525568 | bytes 17253492 | solution.py:564
  505.0 2.2 constant_dynamic-slice_fusion.1
  508.7 2.1 constant_dynamic-slice_fusion.2
  514.6 2.1 copy.65
  516.7 2.4 fusion.236
  519.0 2.1 copy.68
  521.2 2.1 copy.72
  523.4 7.1 convolution_convert_fusion.2
  532.4 24.5 %collective-permute-done = bf16[512,768]{0,1:T(8,128)(2,1)} collective-permute-done((bf16[512,768]{0,1:T(8,128)(2,1)}, bf16[512,768]{0,1:T(8,128)(2,1)}, u32[]{:S(2)}, u32[]{:S(2)}) %collective-permute-start) | collective-permute-done | bytes 786464 | tf_op jit(solution)/shard_map/ppermute | solution.py:572
  564.6 2.1 copy.71
  566.8 2.1 copy.66
  568.9 2.1 copy.67
  571.0 2.1 constant_dynamic-update-slice_fusion.15
  573.1 2.0 constant_dynamic-update-slice_fusion.14
  578.3 5.0 slice_dynamic-update-slice_fusion.3
  583.3 2.5 slice_dynamic-update-slice_fusion.2
  585.8 11.3 %pad_maximum_fusion = bf16[1536,4608]{1,0:T(8,128)(2,1)} fusion(bf16[768,4608]{1,0:T(8,128)(2,1)} %get-tuple-element.271, bf16[768,4608]{1,0:T(8,128)(2,1)} %get-tuple-element.270), kind=kLoop, calls=%fused_computation.65 | loop fusion | flops 28311552 | bytes 28311552 | tf_op jit(solution)/shard_map/concatenate | solution.py:590
  597.4 2.2 fusion.93
  599.7 2.1 fusion.92
  601.8 2.3 add_add_fusion.2
  604.6 153.9 %reduce-scatter.2.cloned.1.call-done = bf16[48,4608]{1,0:T(8,128)(2,1)} async-done(((bf16[1536,4608]{1,0:T(8,128)(2,1)}), bf16[48,4608]{1,0:T(8,128)(2,1)}) %reduce-scatter.2.cloned.1.call-update) | async-done | bytes 442384 | tf_op jit(solution)/shard_map/reduce_scatter | solution.py:597
  764.9 2.2 pad_maximum_fusion.29
  769.1 40.7 %all-reduce = (f32[6]{0:T(128)S(1)}, f32[6]{0:T(128)S(1)}, f32[9216]{0:T(1024)}) all-reduce(f32[6]{0:T(128)S(1)} %pad_maximum_fusion.30, f32[6]{0:T(128)S(1)} %pad_maximum_fusion.29, f32[9216]{0:T(1024)} %copy-done.61), channel_id=1, replica_groups=mesh['dp'=16,'mp'=2] {'dp','mp'}, use_global_device_ids=true, to_apply=%region_37.38 | all-reduce | flops 9228 | bytes 73824 | tf_op jit(solution)/shard_map/psum | solution.py:637
  816.3 2.1 multiply_subtract_fusion.2
  (484 shorter events, 252.2 us)
Async XLA Ops:
  8.0 9.9 %copy-start = (bf16[1,1024,768]{2,1,0:T(8,128)(2,1)S(1)}, bf16[1,1024,768]{2,1,0:T(8,128)(2,1)}, u32[]{:S(2)}) copy-start(bf16[1,1024,768]{2,1,0:T(8,128)(2,1)} %param.30) | copy-start | bytes 4718596
  8.0 10.9 %copy-start.36 = (f32[384,48]{0,1:T(8,128)S(1)}, f32[384,48]{0,1:T(8,128)}, u32[]{:S(2)}) copy-start(f32[384,48]{0,1:T(8,128)} %param.35) | copy-start | bytes 221188
  8.1 75.4 %all-gather.9.cloned.1.call-start = ((), (), s32[]{:S(2)}) async-start(), calls=%async_computation.3 | async-start | bytes 7520256 | tf_op jit(solution)/shard_map/all_gather | solution.py:477
  14.0 105.0 %all-reduce.4.cloned.1.call-start = ((), (), s32[]{:S(2)}) async-start(), calls=%async_computation.4 | async-start | bytes 786432 | tf_op jit(solution)/shard_map/psum | solution.py:501
  17.9 111.0 %copy-start.83 = (s32[128]{0:T(128)}, s32[128]{0:T(128)S(1)}, u32[]{:S(2)}) copy-start(s32[128]{0:T(128)S(1)} %get-tuple-element.310) | copy-start | bytes 1540
  94.6 58.7 %all-reduce.6.cloned.1.call-start = ((), (), s32[]{:S(2)}) async-start(), calls=%async_computation.5 | async-start | bytes 786432 | tf_op jit(solution)/shard_map/psum | solution.py:506
  127.4 26.0 %copy-start.5 = (f32[128,768]{1,0:T(8,128)S(1)}, f32[128,768]{1,0:T(8,128)}, u32[]{:S(2)}) copy-start(f32[128,768]{1,0:T(8,128)} %all-reduce.4.cloned.1.call-done) | copy-start | bytes 1179652
  127.4 106.8 %all-gather.5.cloned.1.call-start = ((), (), s32[]{:S(2)}) async-start(), calls=%async_computation.1 | async-start | bytes 14598144 | tf_op jit(solution)/shard_map/all_gather | solution.py:471
  128.3 476.3 %all-gather.7.cloned.1.call-start = ((), (), s32[]{:S(2)}) async-start(), calls=%async_computation.2 | async-start | bytes 2359296 | tf_op jit(solution)/shard_map/all_gather | solution.py:530
  128.9 206.5 %copy-start.75 = (f32[3072]{0:T(1024)}, f32[3072]{0:T(1024)S(1)}, u32[]{:S(2)}) copy-start(f32[3072]{0:T(1024)S(1)} %slice.225) | copy-start | bytes 36868
  132.6 222.5 %copy-start.73 = (f32[768]{0:T(1024)}, f32[768]{0:T(1024)S(1)}, u32[]{:S(2)}) copy-start(f32[768]{0:T(1024)S(1)} %get-tuple-element.288) | copy-start | bytes 9220
  132.6 222.5 %copy-start.81 = (f32[768]{0:T(1024)}, f32[768]{0:T(1024)S(1)}, u32[]{:S(2)}) copy-start(f32[768]{0:T(1024)S(1)} %get-tuple-element.287) | copy-start | bytes 9220
  154.6 83.6 %copy-start.80 = (f32[128]{0:T(128)}, f32[128]{0:T(128)S(1)}, u32[]{:S(2)}) copy-start(f32[128]{0:T(128)S(1)} %broadcast_multiply_fusion.2) | copy-start | bytes 1540
  238.3 10.4 %copy-start.19 = (bf16[768,384]{1,0:T(8,128)(2,1)}, bf16[768,384]{1,0:T(8,128)(2,1)S(1)}, u32[]{:S(2)}) copy-start(bf16[768,384]{1,0:T(8,128)(2,1)S(1)} %get-tuple-element.264) | copy-start | bytes 1769476
  238.3 10.4 %copy-start.21 = (bf16[768,384]{1,0:T(8,128)(2,1)}, bf16[768,384]{1,0:T(8,128)(2,1)S(1)}, u32[]{:S(2)}) copy-start(bf16[768,384]{1,0:T(8,128)(2,1)S(1)} %get-tuple-element.265) | copy-start | bytes 1769476
  335.1 20.0 %copy-start.3 = (f32[512,768]{1,0:T(8,128)}, f32[512,768]{1,0:T(8,128)S(1)}, u32[]{:S(2)}) copy-start(f32[512,768]{1,0:T(8,128)S(1)} %get-tuple-element.312) | copy-start | bytes 4718596
  335.1 20.0 %copy-start.67 = (f32[512]{0:T(512)}, f32[512]{0:T(512)S(1)}, u32[]{:S(2)}) copy-start(f32[512]{0:T(512)S(1)} %broadcast_multiply_fusion.1) | copy-start | bytes 6148
  335.4 19.6 %copy-start.69 = (f32[512]{0:T(512)}, f32[512]{0:T(512)S(1)}, u32[]{:S(2)}) copy-start(f32[512]{0:T(512)S(1)} %multiply_reduce_fusion.6) | copy-start | bytes 6148
  335.4 19.6 %copy-start.77 = (f32[512]{0:T(512)}, f32[512]{0:T(512)S(1)}, u32[]{:S(2)}) copy-start(f32[512]{0:T(512)S(1)} %fusion.167) | copy-start | bytes 6148
  335.6 19.5 %copy-start.15 = (bf16[768,1536]{1,0:T(8,128)(2,1)S(1)}, bf16[768,1536]{1,0:T(8,128)(2,1)}, u32[]{:S(2)}) copy-start(bf16[768,1536]{1,0:T(8,128)(2,1)} %get-tuple-element.258) | copy-start | bytes 7077892
  335.6 19.5 %copy-start.17 = (bf16[768,1536]{1,0:T(8,128)(2,1)S(1)}, bf16[768,1536]{1,0:T(8,128)(2,1)}, u32[]{:S(2)}) copy-start(bf16[768,1536]{1,0:T(8,128)(2,1)} %get-tuple-element.259) | copy-start | bytes 7077892
  370.9 10.4 %copy-start.35 = (bf16[512,768]{1,0:T(8,128)(2,1)}, bf16[512,768]{1,0:T(8,128)(2,1)S(1)}, u32[]{:S(2)}) copy-start(bf16[512,768]{1,0:T(8,128)(2,1)S(1)} %get-tuple-element.231) | copy-start | bytes 2359300
  507.2 53.7 %collective-permute-start.1 = (bf16[512,768]{0,1:T(8,128)(2,1)}, bf16[512,768]{0,1:T(8,128)(2,1)}, u32[]{:S(2)}, u32[]{:S(2)}) collective-permute-start(bf16[512,768]{0,1:T(8,128)(2,1)} %constant_dynamic-slice_fusion.1), channel_id=1, source_target_pairs={{0,1},{1,0},{2,3},{3,2},{4,5},{5,4},{6,7},{7,6},{8,9},{9,8},{10,11... | collective-permute-start | bytes 2359304 | tf_op jit(solution)/shard_map/ppermute | solution.py:572
  510.8 46.1 %collective-permute-start = (bf16[512,768]{0,1:T(8,128)(2,1)}, bf16[512,768]{0,1:T(8,128)(2,1)}, u32[]{:S(2)}, u32[]{:S(2)}) collective-permute-start(bf16[512,768]{0,1:T(8,128)(2,1)} %constant_dynamic-slice_fusion.2), channel_id=1, source_target_pairs={{0,1},{1,0},{2,3},{3,2},{4,5},{5,4},{6,7},{7,6},{8,9},{9,8},{10,11... | collective-permute-start | bytes 2359304 | tf_op jit(solution)/shard_map/ppermute | solution.py:572
  523.3 235.2 %reduce-scatter.2.cloned.1.call-start = ((), (), s32[]{:S(2)}) async-start(), calls=%async_computation.7 | async-start | bytes 14598144 | tf_op jit(solution)/shard_map/reduce_scatter | solution.py:597
  523.4 33.5 %copy-start.87 = (bf16[1,1024,768]{2,1,0:T(8,128)(2,1)S(1)}, bf16[1,1024,768]{2,1,0:T(8,128)(2,1)}, u32[]{:S(2)}) copy-start(bf16[1,1024,768]{2,1,0:T(8,128)(2,1)} %param.29) | copy-start | bytes 4718596
  530.5 26.4 %copy-start.48 = (bf16[12,1024,64]{1,2,0:T(8,128)(2,1)S(1)}, bf16[12,1024,64]{1,2,0:T(8,128)(2,1)}, u32[]{:S(2)}) copy-start(bf16[12,1024,64]{1,2,0:T(8,128)(2,1)} %get-tuple-element.114) | copy-start | bytes 4718596
  597.1 171.9 %all-gather.11.cloned.1.call-start = ((), (), s32[]{:S(2)}) async-start(), calls=%async_computation.6 | async-start | bytes 4718592 | tf_op jit(solution)/shard_map/all_gather | solution.py:583
  604.1 155.6 %copy-start.37 = (f32[384,48]{0,1:T(8,128)S(1)}, f32[384,48]{0,1:T(8,128)}, u32[]{:S(2)}) copy-start(f32[384,48]{0,1:T(8,128)} %param.35) | copy-start | bytes 221188
  604.1 155.6 %copy-start.59 = (f32[384,48]{0,1:T(8,128)S(1)}, f32[384,48]{0,1:T(8,128)}, u32[]{:S(2)}) copy-start(f32[384,48]{0,1:T(8,128)} %param.39) | copy-start | bytes 221188
  604.1 155.6 %copy-start.60 = (f32[384,48]{0,1:T(8,128)S(1)}, f32[384,48]{0,1:T(8,128)}, u32[]{:S(2)}) copy-start(f32[384,48]{0,1:T(8,128)} %param.43) | copy-start | bytes 221188
  604.1 156.3 %copy-start.28 = (f32[3,48,384]{2,1,0:T(8,128)S(1)}, f32[3,48,384]{2,1,0:T(8,128)}, u32[]{:S(2)}) copy-start(f32[3,48,384]{2,1,0:T(8,128)} %param.34) | copy-start | bytes 663556
  604.1 156.3 %copy-start.56 = (f32[3,48,384]{2,1,0:T(8,128)S(1)}, f32[3,48,384]{2,1,0:T(8,128)}, u32[]{:S(2)}) copy-start(f32[3,48,384]{2,1,0:T(8,128)} %param.38) | copy-start | bytes 663556
  604.1 158.2 %copy-start.10 = (f32[48,1536]{1,0:T(8,128)S(1)}, f32[48,1536]{1,0:T(8,128)}, u32[]{:S(2)}) copy-start(f32[48,1536]{1,0:T(8,128)} %param.36) | copy-start | bytes 884740
  604.2 158.2 %copy-start.52 = (f32[48,1536]{1,0:T(8,128)S(1)}, f32[48,1536]{1,0:T(8,128)}, u32[]{:S(2)}) copy-start(f32[48,1536]{1,0:T(8,128)} %param.40) | copy-start | bytes 884740
  604.2 158.2 %copy-start.53 = (f32[48,1536]{1,0:T(8,128)S(1)}, f32[48,1536]{1,0:T(8,128)}, u32[]{:S(2)}) copy-start(f32[48,1536]{1,0:T(8,128)} %param.44) | copy-start | bytes 884740
  604.5 155.1 %copy-start.61 = (f32[9216]{0:T(1024)}, f32[9216]{0:T(1024)S(1)}, u32[]{:S(2)}) copy-start(f32[9216]{0:T(1024)S(1)} %constant_dynamic-update-slice_fusion.21) | copy-start | bytes 110596
  604.6 158.7 %copy-start.8 = (f32[1536,48]{0,1:T(8,128)S(1)}, f32[1536,48]{0,1:T(8,128)}, u32[]{:S(2)}) copy-start(f32[1536,48]{0,1:T(8,128)} %param.37) | copy-start | bytes 884740
  604.6 158.7 %copy-start.54 = (f32[1536,48]{0,1:T(8,128)S(1)}, f32[1536,48]{0,1:T(8,128)}, u32[]{:S(2)}) copy-start(f32[1536,48]{0,1:T(8,128)} %param.41) | copy-start | bytes 884740
  604.6 158.7 %copy-start.55 = (f32[1536,48]{0,1:T(8,128)S(1)}, f32[1536,48]{0,1:T(8,128)}, u32[]{:S(2)}) copy-start(f32[1536,48]{0,1:T(8,128)} %param.45) | copy-start | bytes 884740
  760.4 55.2 %copy-start.50 = (f32[384,48]{0,1:T(8,128)}, f32[384,48]{0,1:T(8,128)S(1)}, u32[]{:S(2)}) copy-start(f32[384,48]{0,1:T(8,128)S(1)} %get-tuple-element.521) | copy-start | bytes 221188
  760.4 55.2 %copy-start.51 = (f32[384,48]{0,1:T(8,128)}, f32[384,48]{0,1:T(8,128)S(1)}, u32[]{:S(2)}) copy-start(f32[384,48]{0,1:T(8,128)S(1)} %get-tuple-element.525) | copy-start | bytes 221188
  763.3 55.1 %copy-start.30 = (f32[48,1536]{1,0:T(8,128)}, f32[48,1536]{1,0:T(8,128)S(1)}, u32[]{:S(2)}) copy-start(f32[48,1536]{1,0:T(8,128)S(1)} %get-tuple-element.522) | copy-start | bytes 884740
  763.3 55.1 %copy-start.31 = (f32[48,1536]{1,0:T(8,128)}, f32[48,1536]{1,0:T(8,128)S(1)}, u32[]{:S(2)}) copy-start(f32[48,1536]{1,0:T(8,128)S(1)} %get-tuple-element.526) | copy-start | bytes 884740
  763.3 55.1 %copy-start.58 = (f32[9216]{0:T(1024)S(1)}, f32[9216]{0:T(1024)}, u32[]{:S(2)}) copy-start(f32[9216]{0:T(1024)} %param.46) | copy-start | bytes 110596
  764.9 53.6 %copy-start.32 = (f32[1536,48]{0,1:T(8,128)}, f32[1536,48]{0,1:T(8,128)S(1)}, u32[]{:S(2)}) copy-start(f32[1536,48]{0,1:T(8,128)S(1)} %get-tuple-element.523) | copy-start | bytes 884740
  764.9 54.3 %copy-start.29 = (bf16[1024,768]{1,0:T(8,128)(2,1)S(1)}, bf16[1024,768]{1,0:T(8,128)(2,1)}, u32[]{:S(2)}) copy-start(bf16[1024,768]{1,0:T(8,128)(2,1)} %all-gather.7.cloned.1.call-done) | copy-start | bytes 4718596
  809.8 10.5 %copy-start.79 = (f32[6]{0:T(128)}, f32[6]{0:T(128)S(1)}, u32[]{:S(2)}) copy-start(f32[6]{0:T(128)S(1)} %get-tuple-element.532) | copy-start | bytes 76
  (54 other events, 239.1 us)
Sparse Core Ops, SparseCore 0:
  14.1 69.3 all-gather.8
  94.7 24.1 all-reduce.3
  127.6 25.7 all-reduce.5
  523.5 37.5 all-gather.6
  604.3 43.2 all-gather.10
Sparse Core Ops, SparseCore 1:
  131.4 102.8 all-gather.4
  597.2 161.3 reduce-scatter.1

commit v2 on v1

v2 whole, which is shorter than its diff:
```python
from functools import partial

import jax
import jax.numpy as jnp
from jax import lax
from jax.experimental import pallas as pl
from jax.experimental.pallas import tpu as pltpu
from jax.sharding import PartitionSpec as P

HDIM = 64
STEP = 5


beta_one = 0.9
beta_two = 0.999
adam_eps = 1e-06
decay_rate = 0.01
matrix_rate = 0.3
vector_rate = 0.2
cosine_weight = 32.0
cosine_eps = 1e-06
layer_eps = 1e-12
masked_score = -1e30


def layer_norm(row_values, gain_vec, shift_vec):
    center = row_values - jnp.mean(row_values, -1, keepdims=True)
    spread = jnp.mean(center * center, -1, keepdims=True)
    return center * lax.rsqrt(spread + layer_eps) * gain_vec + shift_vec


def vector_parts(packed, model_width):
    pieces = [
        packed[position * model_width : (position + 1) * model_width] for position in range(8)
    ]
    return pieces + [packed[8 * model_width :]]


def head_scores(query, key_rows, visible):
    scale_factor = query.shape[-1] ** (-0.5)
    scores = (
        jnp.einsum("sqe,ske->sqk", query, key_rows, preferred_element_type=jnp.float32)
        * scale_factor
    )
    return jnp.where(visible[:, None, :], scores, masked_score)


def head_forward(query, key_rows, value_rows, visible):
    scores = head_scores(query, key_rows, visible)
    row_peak = jnp.max(scores, -1, keepdims=True)
    exponent = jnp.exp(scores - row_peak)
    row_total = jnp.sum(exponent, -1, keepdims=True)
    weights_low = (exponent / row_total).astype(jnp.bfloat16)
    mixed = jnp.einsum("sqk,ske->sqe", weights_low, value_rows, preferred_element_type=jnp.float32)
    return (mixed.astype(jnp.bfloat16), (row_peak + jnp.log(row_total))[..., 0])


def adam_moments(grad_now, first_old, second_old):
    first_new = beta_one * first_old + (1.0 - beta_one) * grad_now
    second_new = beta_two * second_old + (1.0 - beta_two) * grad_now * grad_now
    step_now = (
        first_new
        / (1.0 - beta_one**STEP)
        / (jnp.sqrt(second_new / (1.0 - beta_two**STEP)) + adam_eps)
    )
    return (first_new, second_new, step_now)


def matrix_squares(attn_w, out_w, up_w, down_w):
    return jnp.concatenate(
        [
            jnp.sum(attn_w * attn_w, axis=(1, 2)),
            jnp.stack([jnp.sum(out_w * out_w), jnp.sum(up_w * up_w), jnp.sum(down_w * down_w)]),
        ]
    )


def shard_pack(attn_w, out_w, up_w, down_w):
    return jnp.concatenate(
        [attn_w[0], attn_w[1], attn_w[2], out_w.T, up_w, down_w.T], axis=1
    )


def cosine_pull(rows, places, aimed, row_start):
    row_count = rows.shape[0]
    local_at = places - row_start
    here = (local_at >= 0) & (local_at < row_count)
    picked = rows[jnp.clip(local_at, 0, row_count - 1)]
    inner = jnp.sum(picked * aimed, -1, keepdims=True)
    square_own = jnp.sum(picked * picked, -1, keepdims=True) + cosine_eps
    square_aim = jnp.sum(aimed * aimed, -1, keepdims=True) + cosine_eps
    inverse = lax.rsqrt(square_own) * lax.rsqrt(square_aim)
    pull = -cosine_weight * (aimed * inverse - picked * (inner * inverse / square_own))
    pull = jnp.where(here[:, None], pull, 0.0)
    return jnp.zeros_like(rows).at[jnp.clip(local_at, 0, row_count - 1)].add(pull)


def heads_of(flat):
    return flat.reshape(flat.shape[0], flat.shape[1] // HDIM, HDIM).transpose(1, 0, 2)


def flat_of(split):
    return split.transpose(1, 0, 2).reshape(split.shape[1], -1)


def dot32(left, right):
    return jnp.dot(left, right, preferred_element_type=jnp.float32)


def dot_nt(left, right):
    return lax.dot_general(
        left, right, (((1,), (1,)), ((), ())), preferred_element_type=jnp.float32
    )


def dot_tn(left, right):
    return lax.dot_general(
        left, right, (((0,), (0,)), ((), ())), preferred_element_type=jnp.float32
    )


def split_rows(
    tokens,
    teacher_tokens,
    cotangent,
    lengths,
    masked,
    attn_weight,
    out_weight,
    up_weight,
    down_weight,
    attn_first,
    out_first,
    up_first,
    down_first,
    attn_second,
    out_second,
    up_second,
    down_second,
    vectors,
    vector_first,
    vector_second,
    teacher_attn,
    teacher_out,
    teacher_up,
    teacher_down,
    teacher_vectors,
):
    low = jnp.bfloat16
    everyone = ("dp", "mp")
    shard_at = lax.axis_index("mp")
    halves = lax.axis_size("mp")
    seq_count, length, width = tokens.shape
    rows = length // halves
    row_start = shard_at * rows
    part = attn_weight.shape[2]
    units = up_weight.shape[1]
    cuts = [0, part, 2 * part, 3 * part, 4 * part, 4 * part + units, 4 * part + 2 * units]
    visible = (jnp.arange(length) < lengths[0])[None, None, :]
    places = masked[0]

    student = lax.all_gather(
        shard_pack(attn_weight, out_weight, up_weight, down_weight).astype(low),
        ("mp", "dp"),
        axis=0,
        tiled=True,
    ).reshape(halves, width, cuts[6])
    teacher = lax.all_gather(
        shard_pack(teacher_attn, teacher_out, teacher_up, teacher_down),
        "dp",
        axis=0,
        tiled=True,
    )

    def whole(index):
        return jnp.concatenate(
            [student[half, :, cuts[index] : cuts[index + 1]] for half in range(halves)], axis=1
        )

    teacher_parts = vector_parts(teacher_vectors.astype(jnp.float32), width)
    bias_q = lax.dynamic_slice_in_dim(teacher_parts[0], shard_at * part, part)
    bias_v = lax.dynamic_slice_in_dim(teacher_parts[1], shard_at * part, part)
    bias_up = lax.dynamic_slice_in_dim(teacher_parts[8], shard_at * units, units)
    teacher_rows = teacher_tokens[0]
    listed = teacher_rows[places]
    t_query = (dot32(listed, teacher[:, : cuts[1]]) + bias_q).astype(low)
    t_keys = dot32(teacher_rows, teacher[:, cuts[1] : cuts[2]]).astype(low)
    t_values = (dot32(teacher_rows, teacher[:, cuts[2] : cuts[3]]) + bias_v).astype(low)
    t_mixed, unused_log = head_forward(
        heads_of(t_query), heads_of(t_keys), heads_of(t_values), visible[0]
    )
    t_branch = lax.psum(dot_nt(flat_of(t_mixed), teacher[:, cuts[3] : cuts[4]]), "mp")
    t_first = listed.astype(jnp.float32) + t_branch + teacher_parts[2]
    t_normed = layer_norm(t_first, teacher_parts[3], teacher_parts[4])
    t_gate = dot32(t_normed.astype(low), teacher[:, cuts[4] : cuts[5]]) + bias_up
    t_act = jax.nn.gelu(t_gate, approximate=False).astype(low)
    t_feed = lax.psum(dot_nt(t_act, teacher[:, cuts[5] : cuts[6]]), "mp")
    aimed = layer_norm(t_normed + t_feed + teacher_parts[5], teacher_parts[6], teacher_parts[7])

    pieces = vector_parts(vectors, width)
    all_rows = tokens[0]
    own_rows = lax.dynamic_slice_in_dim(all_rows, row_start, rows, 0)
    w_q, w_k, w_v, w_out, w_up, w_down = [whole(index) for index in range(6)]
    query = heads_of((dot32(own_rows, w_q) + pieces[0]).astype(low))
    keys = heads_of(dot32(all_rows, w_k).astype(low))
    values = heads_of((dot32(all_rows, w_v) + pieces[1]).astype(low))
    mixed, log_total = lax.map(
        lambda g: jax.tree.map(
            lambda v: v[0], head_forward(g[0][None], g[1][None], g[2][None], visible[0])
        ),
        (query, keys, values),
    )
    attended = flat_of(mixed)
    first_sum = own_rows.astype(jnp.float32) + dot_nt(attended, w_out) + pieces[2]
    normed = layer_norm(first_sum, pieces[3], pieces[4])
    normed_low = normed.astype(low)
    gate_in = dot32(normed_low, w_up) + pieces[8]
    activated = jax.nn.gelu(gate_in, approximate=False).astype(low)
    second_sum = normed + dot_nt(activated, w_down) + pieces[5]
    outcome = layer_norm(second_sum, pieces[6], pieces[7])
    student_out = lax.all_gather(outcome.astype(low), "mp", axis=0, tiled=True)[None]

    own_cotangent = lax.dynamic_slice_in_dim(cotangent[0], row_start, rows, 0)
    grad_top = own_cotangent.astype(jnp.float32) + cosine_pull(outcome, places, aimed, row_start)
    unused_top, pull_top = jax.vjp(layer_norm, second_sum, pieces[6], pieces[7])
    grad_second, grad_gain_two, grad_shift_two = pull_top(grad_top)
    feed_low = grad_second.astype(low)
    grad_down = dot_tn(feed_low, activated)
    grad_act = dot32(feed_low, w_down)
    unused_gelu, pull_gelu = jax.vjp(partial(jax.nn.gelu, approximate=False), gate_in)
    (grad_gate,) = pull_gelu(grad_act)
    gate_low = grad_gate.astype(low)
    grad_up = dot_tn(normed_low, gate_low)
    grad_normed = grad_second + dot_nt(gate_low, w_up)
    unused_mid, pull_mid = jax.vjp(layer_norm, first_sum, pieces[3], pieces[4])
    grad_first, grad_gain_one, grad_shift_one = pull_mid(grad_normed)
    branch_low = grad_first.astype(low)
    grad_out = dot_tn(branch_low, attended)
    grad_heads = heads_of(dot32(branch_low, w_out).astype(low))

    def one_head(g):
        query_h, keys_h, values_h, mixed_h, log_h = g
        scale_factor = HDIM**-0.5
        scores = jnp.where(visible[0], dot_nt(query_h, keys_h) * scale_factor, masked_score)
        probs = jnp.exp(scores - log_h[:, None])
        grad_probs = dot_nt(mixed_h, values_h)
        inner = jnp.sum(probs * grad_probs, -1, keepdims=True)
        grad_scores = (probs * (grad_probs - inner)).astype(low)
        return (
            (dot32(grad_scores, keys_h) * scale_factor).astype(low),
            (dot_tn(grad_scores, query_h) * scale_factor).astype(low),
            dot_tn(probs.astype(low), mixed_h).astype(low),
        )

    grad_query, grad_keys, grad_values = lax.map(
        one_head, (query, keys, values, grad_heads, log_total)
    )
    grad_query = flat_of(grad_query)

    def row_sum(term):
        other = lax.dynamic_slice_in_dim(term, (1 - shard_at) * rows, rows, 0)
        mine = lax.dynamic_slice_in_dim(term, row_start, rows, 0)
        came = lax.ppermute(other, "mp", [(0, 1), (1, 0)])
        return (mine.astype(jnp.float32) + came.astype(jnp.float32)).astype(low)

    grad_keys = row_sum(flat_of(grad_keys))
    grad_values = row_sum(flat_of(grad_values))
    grad_q = dot_tn(own_rows, grad_query)
    grad_k = dot_tn(own_rows, grad_keys)
    grad_v = dot_tn(own_rows, grad_values)
    input_own = (
        grad_first + dot_nt(grad_query, w_q) + dot_nt(grad_keys, w_k) + dot_nt(grad_values, w_v)
    )
    input_grad = lax.all_gather(input_own, "mp", axis=0, tiled=True)[None]

    def half_of(matrix, half):
        span = matrix.shape[1] // halves
        return matrix[:, half * span : (half + 1) * span]

    grads = [grad_q, grad_k, grad_v, grad_out, grad_up, grad_down]
    packed_grad = jnp.concatenate(
        [
            jnp.concatenate([half_of(g, half) for g in grads], axis=1).astype(low)
            for half in range(halves)
        ],
        axis=0,
    )
    summed = lax.psum_scatter(
        packed_grad, ("mp", "dp"), scatter_dimension=0, tiled=True
    ).astype(jnp.float32)
    summed_attn = jnp.stack([summed[:, cuts[i] : cuts[i + 1]] for i in range(3)])
    summed_out = summed[:, cuts[3] : cuts[4]].T
    summed_up = summed[:, cuts[4] : cuts[5]]
    summed_down = summed[:, cuts[5] : cuts[6]].T

    vector_grad = jnp.concatenate(
        [
            jnp.sum(grad_query.astype(jnp.float32), 0),
            jnp.sum(grad_values.astype(jnp.float32), 0),
            jnp.sum(branch_low.astype(jnp.float32), 0),
            grad_gain_one,
            grad_shift_one,
            jnp.sum(feed_low.astype(jnp.float32), 0),
            grad_gain_two,
            grad_shift_two,
            jnp.sum(gate_low.astype(jnp.float32), 0),
        ]
    )
    return (student_out, input_grad) + lamb_update(
        (summed_attn, summed_out, summed_up, summed_down),
        (attn_weight, out_weight, up_weight, down_weight),
        (attn_first, out_first, up_first, down_first),
        (attn_second, out_second, up_second, down_second),
        vector_grad,
        vectors,
        vector_first,
        vector_second,
    )


def lamb_update(grads, weights, firsts, seconds, vector_grad, vectors, vector_first, vector_second):
    moments, squares, steps = [], [], []
    for grad_now, weight, first_old, second_old in zip(grads, weights, firsts, seconds):
        first_new, second_new, step_now = adam_moments(grad_now, first_old, second_old)
        moments.append(first_new)
        squares.append(second_new)
        steps.append(step_now + decay_rate * weight)
    weight_total, update_total, vector_total = lax.psum(
        (matrix_squares(*weights), matrix_squares(*steps), vector_grad), ("dp", "mp")
    )
    weight_norms = jnp.sqrt(weight_total)
    update_norms = jnp.sqrt(update_total)
    trust_ratio = weight_norms / update_norms
    ratios = [trust_ratio[0:3][:, None, None], trust_ratio[3], trust_ratio[4], trust_ratio[5]]
    updated = [
        weight - matrix_rate * ratio * step for weight, ratio, step in zip(weights, ratios, steps)
    ]
    vector_moment, vector_square, step_vector = adam_moments(
        vector_total, vector_first, vector_second
    )
    vector_updated = vectors - vector_rate * step_vector
    return (
        *updated,
        *moments,
        *squares,
        vector_moment,
        vector_square,
        vector_updated,
        jnp.stack([weight_norms, update_norms]),
        trust_ratio,
    )


LOG_PAIR = 128
MESH = pl.DeviceIdType.MESH
low = jnp.bfloat16
f32 = jnp.float32
VMEM_SPEC = pl.BlockSpec(memory_space=pltpu.VMEM)
ANY_SPEC = pl.BlockSpec(memory_space=pl.ANY)
LIMIT = 60 * 2**20


def dnn(left, right):
    return jnp.dot(left, right, preferred_element_type=f32)


def dnt(left, right):
    return lax.dot_general(left, right, (((1,), (1,)), ((), ())), preferred_element_type=f32)


def lane_index(shape):
    return lax.broadcasted_iota(jnp.int32, shape, 1)


def split_three(value):
    top = value.astype(low).astype(f32)
    rest = value - top
    middle = rest.astype(low).astype(f32)
    return (top, middle, rest - middle)


def flip(value):
    return value.astype(f32).T.astype(low)


def place():
    at = lax.axis_index("dp")
    return (at, lax.axis_index("mp"), at // 4, (at // 2) % 2, at % 2)


def near():
    at, y, z, x, core = place()
    return dict(
        twin=(at + 1 - 2 * core, y),
        x=(at + 2 - 4 * x, y),
        y=(at, 1 - y),
        z=[(((z + step) % 4) * 4 + 2 * x + core, y) for step in (1, 2, 3)],
    )


def greet(peers):
    sem = pltpu.get_barrier_semaphore()
    for peer in peers:
        pl.semaphore_signal(sem, inc=1, device_id=peer, device_id_type=MESH)
    pl.semaphore_wait(sem, len(peers))


def remote(src, dst, sends, recvs, at, peer):
    return pltpu.make_async_remote_copy(
        src_ref=src,
        dst_ref=dst,
        send_sem=sends.at[at],
        recv_sem=recvs.at[at],
        device_id=peer,
        device_id_type=MESH,
    )


def row_norm(rows):
    center = rows - jnp.mean(rows, -1, keepdims=True)
    scale = lax.rsqrt(jnp.mean(center * center, -1, keepdims=True) + layer_eps)
    return (center * scale, scale)


def norm_pull(grad, unit, scale, gain):
    lifted = grad * gain
    return scale * (
        lifted
        - jnp.mean(lifted, -1, keepdims=True)
        - unit * jnp.mean(lifted * unit, -1, keepdims=True)
    )


def normal_share(value):
    return 0.5 * (1.0 + lax.erf(value * 0.7071067811865476))


def pair_forward(query, keys, values, bias):
    count, span = query.shape[0], keys.shape[0]
    lane_q, lane_k = lane_index((count, LOG_PAIR)), lane_index((span, LOG_PAIR))
    outs, logs = [], []
    for head in range(2):
        spare = HDIM * (1 - head)
        keys_now = jnp.where(
            lane_k // HDIM == head,
            keys.astype(f32),
            jnp.where(lane_k == spare, bias, 0.0),
        ).astype(low)
        query_now = jnp.where(
            lane_q // HDIM == head,
            query.astype(f32),
            jnp.where(lane_q == spare, 1.0, 0.0),
        ).astype(low)
        scores = dnt(query_now, keys_now)
        peak = jnp.max(scores, -1, keepdims=True)
        exponent = jnp.exp(scores - peak)
        total = jnp.sum(exponent, -1, keepdims=True)
        outs.append(dnn((exponent * (1.0 / total)).astype(low), values))
        logs.append(peak + jnp.log(total))
    return (
        jnp.where(lane_q < HDIM, outs[0], outs[1]),
        jnp.where(lane_q < HDIM, logs[0], logs[1]),
    )


def project_rows(x_ref, w_ref, vec_ref, y, q_ref, k_ref, v_ref):
    length, width = x_ref.shape
    part = width // 2
    block = 256

    def keys_values(step, carry):
        at = pl.ds(pl.multiple_of(step * block, block), block)
        rows = x_ref[at, :]
        for half in range(2):
            cols = slice(half * part, (half + 1) * part)
            k_ref[at, cols] = dnn(rows, w_ref[half, :, part : 2 * part]).astype(low)
            v_ref[at, cols] = (
                dnn(rows, w_ref[half, :, 2 * part : 3 * part]) + vec_ref[1:2, cols]
            ).astype(low)
        return carry

    lax.fori_loop(0, length // block, keys_values, 0)

    def queries(step, carry):
        at = pl.ds(pl.multiple_of(step * block, block), block)
        rows = x_ref[pl.ds(pl.multiple_of(y * (length // 2) + step * block, block), block), :]
        for half in range(2):
            cols = slice(half * part, (half + 1) * part)
            q_ref[at, cols] = (
                (dnn(rows, w_ref[half, :, 0:part]) + vec_ref[0:1, cols]).astype(low).astype(f32)
                * HDIM**-0.5
            ).astype(low)
        return carry

    lax.fori_loop(0, length // 2 // block, queries, 0)


def attend_rows(q_ref, k_ref, v_ref, bias_ref, a_ref, af_ref, log_ref):
    block = 256
    rows = q_ref.shape[0]

    def one_pair(pair, carry):
        cols = pl.ds(pl.multiple_of(pair * LOG_PAIR, LOG_PAIR), LOG_PAIR)
        keys, values, bias = k_ref[:, cols], v_ref[:, cols], bias_ref[...]
        for start in range(0, rows, block):
            at = slice(start, start + block)
            mixed, logs = pair_forward(q_ref[at, cols], keys, values, bias)
            a_ref[at, cols] = mixed.astype(low)
            af_ref[at, cols] = mixed
            log_ref[pair, at, :] = logs
        return carry

    lax.fori_loop(0, q_ref.shape[1] // LOG_PAIR, one_pair, 0)


def feed_rows(x_ref, a_ref, w_ref, vec_ref, y, r1_ref, z_ref, u_ref, r2_ref, out_ref):
    rows, width = a_ref.shape
    part = width // 2
    block = 256

    def some_rows(step, carry):
        at = pl.ds(pl.multiple_of(step * block, block), block)
        x_at = pl.ds(pl.multiple_of(y * rows + step * block, block), block)
        first = x_ref[x_at, :].astype(f32) + vec_ref[2:3, :]
        for half in range(2):
            first += dnt(
                a_ref[at, half * part : (half + 1) * part], w_ref[half, :, 3 * part : 4 * part]
            )
        r1_ref[at, :] = first
        unit, unused = row_norm(first)
        normed = unit * vec_ref[3:4, :] + vec_ref[4:5, :]
        normed_low = normed.astype(low)
        r2_ref[at, :] = normed + vec_ref[5:6, :]
        for piece in range(4):
            half, base = piece // 2, 4 * part + (piece % 2) * width
            cols = slice(piece * width, (piece + 1) * width)
            gate = dnn(normed_low, w_ref[half, :, base : base + width]) + vec_ref[
                8 + piece : 9 + piece, :
            ]
            z_ref[at, cols] = gate
            active = (gate * normal_share(gate)).astype(low)
            u_ref[at, cols] = active
            r2_ref[at, :] += dnt(active, w_ref[half, :, base + 2 * width : base + 3 * width])
        unit, unused = row_norm(r2_ref[at, :])
        out_ref[at, :] = unit * vec_ref[6:7, :] + vec_ref[7:8, :]
        return carry

    lax.fori_loop(0, rows // block, some_rows, 0)


def forward_kernel(
    x_ref, w_ref, vec_ref, bias_ref,
    q_ref, k_ref, v_ref, a_ref, af_ref, log_ref, r1_ref, z_ref, u_ref, r2_ref, out_ref,
):
    y = lax.axis_index("mp")
    project_rows(x_ref, w_ref, vec_ref, y, q_ref, k_ref, v_ref)
    attend_rows(q_ref, k_ref, v_ref, bias_ref, a_ref, af_ref, log_ref)
    feed_rows(x_ref, a_ref, w_ref, vec_ref, y, r1_ref, z_ref, u_ref, r2_ref, out_ref)


def shape_of(*dims, kind=f32):
    return jax.ShapeDtypeStruct(dims, kind)


def forward_call(x, w, vec, bias):
    length, width = x.shape
    rows = length // 2
    hidden = 4 * width
    return pl.pallas_call(
        forward_kernel,
        name="student_forward",
        out_shape=[
            shape_of(rows, width, kind=low),
            shape_of(length, width, kind=low),
            shape_of(length, width, kind=low),
            shape_of(rows, width, kind=low),
            shape_of(rows, width),
            shape_of(width // LOG_PAIR, rows, LOG_PAIR),
            shape_of(rows, width),
            shape_of(rows, hidden),
            shape_of(rows, hidden, kind=low),
            shape_of(rows, width),
            shape_of(rows, width),
        ],
        in_specs=[VMEM_SPEC] * 4,
        out_specs=[VMEM_SPEC] * 11,
        compiler_params=pltpu.CompilerParams(vmem_limit_bytes=LIMIT),
    )(x, w, vec, bias)


def teacher_kernel(
    x_ref, w_ref, vec_ref, bias_ref, places_ref, aimed_ref, k_ref, v_ref, part_ref, come_ref,
    sends, recvs,
):
    y = lax.axis_index("mp")
    peer = near()["y"]
    greet([peer])
    length, width = x_ref.shape
    part = width // 2
    count = places_ref.shape[0]
    mine = pl.ds(pl.multiple_of(y * part, LOG_PAIR), part)
    block = 256

    def keys_values(step, carry):
        at = pl.ds(pl.multiple_of(step * block, block), block)
        rows = x_ref[at, :]
        k_ref[at, :] = dnn(rows, w_ref[:, part : 2 * part]).astype(low)
        v_ref[at, :] = (dnn(rows, w_ref[:, 2 * part : 3 * part]) + vec_ref[1:2, mine]).astype(low)
        return carry

    lax.fori_loop(0, length // block, keys_values, 0)
    pick = jnp.where(places_ref[:, 0:1] == lane_index((count, length)), 1.0, 0.0).astype(low)
    listed = dnn(pick, x_ref[...])
    query = (dnn(listed.astype(low), w_ref[:, 0:part]) + vec_ref[0:1, mine]).astype(low)
    query = (query.astype(f32) * HDIM**-0.5).astype(low)
    branch = jnp.zeros((count, width), f32)
    for pair in range(part // LOG_PAIR):
        cols = slice(pair * LOG_PAIR, (pair + 1) * LOG_PAIR)
        mixed, unused = pair_forward(query[:, cols], k_ref[:, cols], v_ref[:, cols], bias_ref[...])
        branch += dnt(mixed.astype(low), w_ref[:, 3 * part + pair * LOG_PAIR : 3 * part + (pair + 1) * LOG_PAIR])

    def joined(value, at):
        part_ref[at] = value
        copy = remote(part_ref.at[at], come_ref.at[at], sends, recvs, at, peer)
        copy.start()
        copy.wait()
        return value + come_ref[at]

    first = listed + joined(branch, 0) + vec_ref[2:3, :]
    unit, unused = row_norm(first)
    normed = unit * vec_ref[3:4, :] + vec_ref[4:5, :]
    normed_low = normed.astype(low)
    feed = jnp.zeros((count, width), f32)
    for piece in range(2):
        base = 4 * part + piece * width
        gate = dnn(normed_low, w_ref[:, base : base + width])
        gate += vec_ref[pl.ds(8 + 2 * y + piece, 1), :]
        active = (gate * normal_share(gate)).astype(low)
        feed += dnt(active, w_ref[:, base + 2 * width : base + 3 * width])
    second = normed + joined(feed, 1) + vec_ref[5:6, :]
    unit, unused = row_norm(second)
    aimed_ref[...] = unit * vec_ref[6:7, :] + vec_ref[7:8, :]


def teacher_call(x, w, vec, bias, places, number):
    length, width = x.shape
    count = places.shape[0]
    return pl.pallas_call(
        teacher_kernel,
        name="teacher_forward",
        out_shape=shape_of(count, width),
        in_specs=[VMEM_SPEC] * 5,
        out_specs=VMEM_SPEC,
        scratch_shapes=[
            pltpu.VMEM((length, width // 2), low),
            pltpu.VMEM((length, width // 2), low),
            pltpu.VMEM((2, count, width), f32),
            pltpu.VMEM((2, count, width), f32),
            pltpu.SemaphoreType.DMA((2,)),
            pltpu.SemaphoreType.DMA((2,)),
        ],
        compiler_params=pltpu.CompilerParams(
            vmem_limit_bytes=LIMIT, collective_id=number, has_side_effects=True
        ),
    )(x, w, vec, bias, places)


def feed_back_kernel(
    out_ref, cot_ref, aimed_ref, places_ref, r1_ref, r2_ref, z_ref, u_ref, a_ref, w_ref, vec_ref,
    grad_ref, ga_ref, g1_ref, sums_ref, flipped_ref, normed_flip_ref, gr2_ref,
):
    y = lax.axis_index("mp")
    rows, width = out_ref.shape
    part = width // 2
    block = 256
    sums_ref[...] = jnp.zeros(sums_ref.shape, f32)

    def top(step, carry):
        at = pl.ds(pl.multiple_of(step * block, block), block)
        row_at = lax.broadcasted_iota(jnp.int32, (block, places_ref.shape[1]), 0)
        pick = jnp.where(row_at + (y * rows + step * block) == places_ref[0:1, :], 1.0, 0.0)
        times = jnp.sum(pick, -1, keepdims=True)
        aimed = jnp.dot(
            pick, aimed_ref[...], precision=lax.Precision.HIGHEST, preferred_element_type=f32
        ) / jnp.maximum(times, 1.0)
        own = out_ref[at, :]
        inner = jnp.sum(own * aimed, -1, keepdims=True)
        square_own = jnp.sum(own * own, -1, keepdims=True) + cosine_eps
        square_aim = jnp.sum(aimed * aimed, -1, keepdims=True) + cosine_eps
        scale = cosine_weight * times * lax.rsqrt(square_own) * lax.rsqrt(square_aim)
        grad = cot_ref[at, :].astype(f32) - scale * (aimed - own * (inner / square_own))
        unit, spread = row_norm(r2_ref[at, :])
        sums_ref[6:7, :] += jnp.sum(grad * unit, 0, keepdims=True)
        sums_ref[7:8, :] += jnp.sum(grad, 0, keepdims=True)
        back = norm_pull(grad, unit, spread, vec_ref[6:7, :])
        gr2_ref[at, :] = back
        back_low = back.astype(low)
        sums_ref[5:6, :] += jnp.sum(back_low.astype(f32), 0, keepdims=True)
        ga_ref[at, :] = back_low
        flipped_ref[:, at] = flip(back_low)
        unit, unused = row_norm(r1_ref[at, :])
        normed_flip_ref[:, at] = flip(unit * vec_ref[3:4, :] + vec_ref[4:5, :])
        return carry

    lax.fori_loop(0, rows // block, top, 0)
    feed_low = ga_ref[...]
    for piece in range(4):
        half, base = piece // 2, 4 * part + (piece % 2) * width
        up_cols = slice(base, base + width)
        down_cols = slice(base + 2 * width, base + 3 * width)
        cols = slice(piece * width, (piece + 1) * width)
        grad_ref[half, :, down_cols] = dnn(flipped_ref[...], u_ref[:, cols]).astype(low)
        gate = z_ref[:, cols]
        slope = normal_share(gate) + gate * (
            jnp.exp(-0.5 * gate * gate) * 0.3989422804014327
        )
        gate_low = (dnn(feed_low, w_ref[half, :, down_cols]) * slope).astype(low)
        sums_ref[8 + piece : 9 + piece, :] = jnp.sum(gate_low.astype(f32), 0, keepdims=True)
        grad_ref[half, :, up_cols] = dnn(normed_flip_ref[...], gate_low).astype(low)
        gr2_ref[...] += dnt(gate_low, w_ref[half, :, up_cols])

    def middle(step, carry):
        at = pl.ds(pl.multiple_of(step * block, block), block)
        grad = gr2_ref[at, :]
        unit, spread = row_norm(r1_ref[at, :])
        sums_ref[3:4, :] += jnp.sum(grad * unit, 0, keepdims=True)
        sums_ref[4:5, :] += jnp.sum(grad, 0, keepdims=True)
        back = norm_pull(grad, unit, spread, vec_ref[3:4, :])
        g1_ref[at, :] = back
        back_low = back.astype(low)
        sums_ref[2:3, :] += jnp.sum(back_low.astype(f32), 0, keepdims=True)
        flipped_ref[:, at] = flip(back_low)
        for half in range(2):
            cols = slice(half * part, (half + 1) * part)
            ga_ref[at, cols] = dnn(back_low, w_ref[half, :, 3 * part : 4 * part]).astype(low)
        return carry

    lax.fori_loop(0, rows // block, middle, 0)
    for half in range(2):
        grad_ref[half, :, 3 * part : 4 * part] = dnn(
            flipped_ref[...], a_ref[:, half * part : (half + 1) * part]
        ).astype(low)


def feed_back_call(out, cot, aimed, places, r1, r2, z, u, a, w, vec):
    rows, width = out.shape
    return pl.pallas_call(
        feed_back_kernel,
        name="feed_backward",
        out_shape=[
            shape_of(*w.shape, kind=low),
            shape_of(rows, width, kind=low),
            shape_of(rows, width),
            shape_of(*vec.shape),
        ],
        in_specs=[VMEM_SPEC] * 11,
        out_specs=[VMEM_SPEC] * 4,
        scratch_shapes=[
            pltpu.VMEM((width, rows), low),
            pltpu.VMEM((width, rows), low),
            pltpu.VMEM((rows, width), f32),
        ],
        compiler_params=pltpu.CompilerParams(vmem_limit_bytes=LIMIT),
    )(out, cot, aimed, places, r1, r2, z, u, a, w, vec)


def pair_back(query, grad_mixed, mixed, logs, keys, values, bias):
    count, span = query.shape[0], keys.shape[0]
    lane_q, lane_k = lane_index((count, LOG_PAIR)), lane_index((span, LOG_PAIR))
    query_wide, grad_wide = query.astype(f32), grad_mixed.astype(f32)
    keys_wide, values_wide = keys.astype(f32), values.astype(f32)
    product = grad_wide * mixed
    grad_keys, grad_values, grad_query = [], [], []
    for head in range(2):
        spare = HDIM * (1 - head)
        own_q, own_k = lane_q // HDIM == head, lane_k // HDIM == head
        inner = jnp.sum(jnp.where(own_q, product, 0.0), -1, keepdims=True)
        query_now = jnp.where(own_q, query_wide, jnp.where(lane_q == spare, 1.0, 0.0))
        grad_now = jnp.where(own_q, grad_wide, 0.0)
        for place_at, (log_term, inner_term) in enumerate(
            zip(split_three(logs[:, HDIM * head : HDIM * head + 1]), split_three(inner))
        ):
            here = lane_q == spare + 1 + place_at
            query_now = jnp.where(here, log_term, query_now)
            grad_now = jnp.where(here, inner_term, grad_now)
        minus = jnp.where((lane_k > spare) & (lane_k < spare + 4), -1.0, 0.0)
        keys_now = jnp.where(own_k, keys_wide, jnp.where(lane_k == spare, bias, minus)).astype(low)
        values_now = jnp.where(own_k, values_wide, minus).astype(low)
        probs = jnp.exp(dnt(keys_now, query_now.astype(low)))
        grad_scores = (probs * dnt(values_now, grad_now.astype(low))).astype(low)
        grad_keys.append(dnn(grad_scores, query))
        grad_values.append(dnn(probs.astype(low), grad_mixed))
        flipped = keys_wide.T[HDIM * head : HDIM * (head + 1)].astype(low)
        grad_query.append(dnn(flipped, grad_scores))
    return (
        jnp.concatenate(grad_query, 0).T * HDIM**-0.5,
        jnp.where(lane_k < HDIM, grad_keys[0], grad_keys[1]),
        jnp.where(lane_k < HDIM, grad_values[0], grad_values[1]),
    )


def attend_back_kernel(
    x_ref, q_ref, k_ref, v_ref, bias_ref, log_ref, af_ref, ga_ref, g1_ref, out_ref, w_ref,
    grad_ref, input_ref, student_ref, sums_ref,
    gq_ref, gk_ref, gv_ref, come_ref, x_flip_ref, send_ref, come_in_ref, sends, recvs,
):
    y = lax.axis_index("mp")
    peer = near()["y"]
    greet([peer])
    rows, width = q_ref.shape
    part = width // 2
    own = pl.ds(pl.multiple_of(y * rows, rows), rows)
    other = pl.ds(pl.multiple_of((1 - y) * rows, rows), rows)
    student_ref[own, :] = out_ref[...].astype(low)
    share = remote(student_ref.at[own], student_ref.at[own], sends, recvs, 0, peer)
    share.start()
    x_flip_ref[...] = flip(x_ref[own, :])

    def one_pair(pair, carry):
        cols = pl.ds(pl.multiple_of(pair * LOG_PAIR, LOG_PAIR), LOG_PAIR)
        grad_query, grad_keys, grad_values = pair_back(
            q_ref[:, cols], ga_ref[:, cols], af_ref[:, cols], log_ref[pair],
            k_ref[:, cols], v_ref[:, cols], bias_ref[...],
        )
        gq_ref[:, cols] = grad_query.astype(low)
        gk_ref[:, cols] = grad_keys.astype(low)
        gv_ref[:, cols] = grad_values.astype(low)
        return carry

    lax.fori_loop(0, width // LOG_PAIR, one_pair, 0)
    copies = [
        remote(source.at[other], come_ref.at[at], sends, recvs, 1 + at, peer)
        for at, source in enumerate((gk_ref, gv_ref))
    ]
    for copy in copies:
        copy.start()
    sums_ref[...] = jnp.zeros(sums_ref.shape, f32)
    sums_ref[0:1, :] = jnp.sum(gq_ref[...].astype(f32), 0, keepdims=True)

    def weight_grad(base, value_ref):
        for half in range(2):
            grad_ref[half, :, base : base + part] = dnn(
                x_flip_ref[...], value_ref[:, half * part : (half + 1) * part]
            ).astype(low)

    def input_part(base, value_ref):
        total = dnt(value_ref[:, 0:part], w_ref[0, :, base : base + part])
        return total + dnt(value_ref[:, part:width], w_ref[1, :, base : base + part])

    weight_grad(0, gq_ref)
    total = g1_ref[...] + input_part(0, gq_ref)
    for at, source in enumerate((gk_ref, gv_ref)):
        copies[at].wait()
        gq_ref[...] = (source[own, :].astype(f32) + come_ref[at].astype(f32)).astype(low)
        weight_grad((1 + at) * part, gq_ref)
        total += input_part((1 + at) * part, gq_ref)
    sums_ref[1:2, :] = jnp.sum(gq_ref[...].astype(f32), 0, keepdims=True)
    input_ref[own, :] = total
    send_ref[...] = total.astype(low)
    copy = remote(send_ref, come_in_ref, sends, recvs, 3, peer)
    copy.start()
    copy.wait()
    input_ref[other, :] = come_in_ref[...].astype(f32)
    share.wait_send()
    remote(student_ref.at[other], student_ref.at[other], sends, recvs, 0, peer).wait_recv()


def attend_back_call(x, q, k, v, bias, logs, af, ga, g1, out, w, number):
    length, width = x.shape
    rows = length // 2
    return pl.pallas_call(
        attend_back_kernel,
        name="attention_backward",
        out_shape=[
            shape_of(2, width, 3 * width // 2, kind=low),
            shape_of(length, width),
            shape_of(length, width, kind=low),
            shape_of(12, width),
        ],
        in_specs=[VMEM_SPEC] * 11,
        out_specs=[VMEM_SPEC] * 4,
        scratch_shapes=[
            pltpu.VMEM((rows, width), low),
            pltpu.VMEM((length, width), low),
            pltpu.VMEM((length, width), low),
            pltpu.VMEM((2, rows, width), low),
            pltpu.VMEM((width, rows), low),
            pltpu.VMEM((rows, width), low),
            pltpu.VMEM((rows, width), low),
            pltpu.SemaphoreType.DMA((4,)),
            pltpu.SemaphoreType.DMA((4,)),
        ],
        compiler_params=pltpu.CompilerParams(
            vmem_limit_bytes=LIMIT, collective_id=number, has_side_effects=True
        ),
    )(x, q, k, v, bias, logs, af, ga, g1, out, w)


def adam_step(grad, first, second):
    first_new = beta_one * first + (1.0 - beta_one) * grad
    second_new = beta_two * second + (1.0 - beta_two) * grad * grad
    step = (
        first_new
        / (1.0 - beta_one**STEP)
        / (jnp.sqrt(second_new / (1.0 - beta_two**STEP)) + adam_eps)
    )
    return (first_new, second_new, step)


def shared_sum(value, mine_ref, come_ref, sends, recvs, ways, z):
    for at, way in enumerate(("twin", "x", "y")):
        mine_ref[at] = value
        copy = remote(mine_ref.at[at], come_ref.at[at], sends, recvs, at, ways[way])
        copy.start()
        copy.wait()
        value = value + come_ref[at]
    mine_ref[3] = value
    copies = []
    for step in range(3):
        copy = remote(mine_ref.at[3], come_ref.at[3 + step], sends, recvs, 3 + step, ways["z"][step])
        copy.start()
        copies.append(copy)
    for copy in copies:
        copy.wait()
    terms = [value] + [come_ref[3 + step] for step in range(3)]
    total = None
    for z_from in range(4):
        term = terms[0]
        for step in range(1, 4):
            term = jnp.where((z + 4 - step) % 4 == z_from, terms[step], term)
        total = term if total is None else total + term
    return total


def finish_kernel(
    chunks,
    ga_ref, gf_ref, vg_ref, vec_ref, vm_ref, vs_ref,
    aw, ow, uw, dw, am, om, um, dm, a2, o2, u2, d2,
    aw_o, ow_o, uw_o, dw_o, am_o, om_o, um_o, dm_o, a2_o, o2_o, u2_o, d2_o,
    vm_o, vs_o, vec_o, norm_o,
    one_ref, ax_ref, ay_ref, bx_ref, by_ref, z_ref, tot_ref, vmine, vcome, nmine, ncome,
    sends, recvs, zsends, zrecvs, vsends, vrecvs, nsends, nrecvs,
):
    at, y, z, x, core = place()
    ways = near()
    greet([ways["twin"], ways["x"], ways["y"]] + ways["z"])
    part = aw.shape[2]
    units = uw.shape[1]
    low_half, high_half = pl.ds(0, 2), pl.ds(2, 2)
    started = []

    def go(src, dst, kind, chunk, peer):
        copy = remote(src, dst, sends, recvs, (chunk, kind), peer)
        copy.start()
        started.append(copy)

    def landed(dst, kind, chunk):
        remote(dst, dst, sends, recvs, (chunk, kind), ways["x"]).wait_recv()

    def source(chunk):
        a, b = chunks[chunk]
        if b <= 3 * part:
            return (ga_ref, pl.ds(a, b - a))
        return (gf_ref, pl.ds(a, b - a))

    def cols(chunk):
        a, b = chunks[chunk]
        return pl.ds(a, b - a)

    for k in range(len(chunks)):
        ref, span = source(k)
        go(ref.at[:, :, :, 1 - core, :, span], one_ref.at[:, :, :, :, cols(k)], 0, k, ways["twin"])
    vector_total = shared_sum(vg_ref[...], vmine, vcome, vsends, vrecvs, ways, z)
    for k in range(len(chunks)):
        ref, span = source(k)
        here = cols(k)
        landed(one_ref.at[:, :, :, :, here], 0, k)

        def add_block(step, carry, ref=ref, span=span, here=here):
            yy, zz, xx = step // 8, (step // 2) % 4, step % 2
            one_ref[yy, zz, xx, :, here] = (
                one_ref[yy, zz, xx, :, here].astype(f32) + ref[yy, zz, xx, core, :, span].astype(f32)
            ).astype(low)
            return carry

        lax.fori_loop(0, 16, add_block, 0)
        go(one_ref.at[:, low_half, 1 - x, :, here], ax_ref.at[:, :, :, here], 1, k, ways["x"])
        go(one_ref.at[1 - y, high_half, :, :, here], by_ref.at[:, :, :, here], 2, k, ways["y"])
    for k in range(len(chunks)):
        here = cols(k)
        landed(ax_ref.at[:, :, :, here], 1, k)

        def add_x(step, carry, here=here):
            yy, zz = step // 2, step % 2
            ax_ref[yy, zz, :, here] = (
                ax_ref[yy, zz, :, here].astype(f32) + one_ref[yy, zz, x, :, here].astype(f32)
            ).astype(low)
            return carry

        lax.fori_loop(0, 4, add_x, 0)
        go(ax_ref.at[1 - y, :, :, here], ay_ref.at[:, :, here], 3, k, ways["y"])
        landed(by_ref.at[:, :, :, here], 2, k)

        def add_y(step, carry, here=here):
            zz, xx = step // 2, step % 2
            by_ref[zz, xx, :, here] = (
                by_ref[zz, xx, :, here].astype(f32) + one_ref[y, 2 + zz, xx, :, here].astype(f32)
            ).astype(low)
            return carry

        lax.fori_loop(0, 4, add_y, 0)
        go(by_ref.at[:, 1 - x, :, here], bx_ref.at[:, :, here], 4, k, ways["x"])
    zcopies = []
    for k in range(len(chunks)):
        here = cols(k)
        landed(ay_ref.at[:, :, here], 3, k)
        landed(bx_ref.at[:, :, here], 4, k)
        for zz in range(2):
            tot_ref[zz, :, here] = (
                ax_ref[y, zz, :, here].astype(f32) + ay_ref[zz, :, here].astype(f32)
            ).astype(low)
            tot_ref[2 + zz, :, here] = (
                by_ref[zz, x, :, here].astype(f32) + bx_ref[zz, :, here].astype(f32)
            ).astype(low)
        for step in range(3):
            copy = remote(
                tot_ref.at[(z + 1 + step) % 4, :, here], z_ref.at[step, :, here],
                zsends, zrecvs, (k, step), ways["z"][step],
            )
            copy.start()
            zcopies.append(copy)
    for copy in zcopies:
        copy.wait()
    for copy in started:
        copy.wait_send()

    def grad_of(a, b):
        total = tot_ref[z, :, a:b].astype(f32)
        for step in range(3):
            total += z_ref[step, :, a:b].astype(f32)
        return total

    lane = lane_index((8, LOG_PAIR))
    row = lax.broadcasted_iota(jnp.int32, (8, LOG_PAIR), 0)
    squares = jnp.zeros((8, LOG_PAIR), f32)

    def one_matrix(index, grad, w, first, second, w_o, first_o, second_o, squares):
        first_new, second_new, step = adam_step(grad, first[...], second[...])
        first_o[...] = first_new
        second_o[...] = second_new
        weight = w[...]
        step = step + decay_rate * weight
        w_o[...] = step
        for line, value in ((0, weight), (1, step)):
            total = jnp.sum(jnp.sum(value * value, -1, keepdims=True), 0, keepdims=True)
            squares = jnp.where((row == line) & (lane == index), total, squares)
        return squares

    for index in range(3):
        squares = one_matrix(
            index, grad_of(index * part, (index + 1) * part), aw.at[index], am.at[index], a2.at[index],
            aw_o.at[index], am_o.at[index], a2_o.at[index], squares,
        )
    squares = one_matrix(
        3, grad_of(3 * part, 4 * part), ow, om, o2, ow_o, om_o, o2_o, squares
    )
    squares = one_matrix(
        4, grad_of(4 * part, 4 * part + units), uw, um, u2, uw_o, um_o, u2_o, squares
    )
    squares = one_matrix(
        5, grad_of(4 * part + units, 4 * part + 2 * units), dw, dm, d2, dw_o, dm_o, d2_o, squares
    )
    vm_new, vs_new, vector_step = adam_step(vector_total, vm_ref[...], vs_ref[...])
    vm_o[...] = vm_new
    vs_o[...] = vs_new
    vec_o[...] = vec_ref[...] - vector_rate * vector_step
    norms = jnp.sqrt(shared_sum(squares, nmine, ncome, nsends, nrecvs, ways, z))
    ratio = norms[0:1, :] / norms[1:2, :]
    norm_o[...] = jnp.where(row == 2, ratio, norms)

    def apply(index, w, w_o):
        w_o[...] = w[...] - matrix_rate * ratio[0:1, index : index + 1] * w_o[...]

    for index in range(3):
        apply(index, aw.at[index], aw_o.at[index])
    apply(3, ow, ow_o)
    apply(4, uw, uw_o)
    apply(5, dw, dw_o)


def finish_call(grad_attn, grad_feed, vector_grad, vec, vm, vs, weights, firsts, seconds, number):
    part = weights[0].shape[2]
    units = weights[2].shape[1]
    lines = weights[0].shape[1]
    wide = 4 * part + 2 * units
    chunks = (
        (4 * part, 4 * part + units), (4 * part + units, wide), (3 * part, 4 * part), (0, 3 * part),
    )
    count = len(chunks)
    outs = [shape_of(*v.shape) for group in (weights, firsts, seconds) for v in group]
    outs += [shape_of(*vec.shape)] * 3 + [shape_of(8, LOG_PAIR)]
    sem = pltpu.SemaphoreType.DMA
    return pl.pallas_call(
        partial(finish_kernel, chunks),
        name="sum_and_update",
        out_shape=outs,
        in_specs=[VMEM_SPEC] * 18,
        out_specs=[VMEM_SPEC] * len(outs),
        scratch_shapes=[
            pltpu.VMEM((2, 4, 2, lines, wide), low),
            pltpu.VMEM((2, 2, lines, wide), low),
            pltpu.VMEM((2, lines, wide), low),
            pltpu.VMEM((2, lines, wide), low),
            pltpu.VMEM((2, 2, lines, wide), low),
            pltpu.VMEM((3, lines, wide), low),
            pltpu.VMEM((4, lines, wide), low),
            pltpu.VMEM((4,) + vec.shape, f32),
            pltpu.VMEM((6,) + vec.shape, f32),
            pltpu.VMEM((4, 8, LOG_PAIR), f32),
            pltpu.VMEM((6, 8, LOG_PAIR), f32),
            sem((count, 5)), sem((count, 5)), sem((count, 3)), sem((count, 3)),
            sem((6,)), sem((6,)), sem((6,)), sem((6,)),
        ],
        compiler_params=pltpu.CompilerParams(
            vmem_limit_bytes=LIMIT, collective_id=number, has_side_effects=True
        ),
    )(grad_attn, grad_feed, vector_grad, vec, vm, vs, *weights, *firsts, *seconds)


def gather_kernel(
    own_cuts, aim_cuts, ps_ref, pt_ref, gs_ref, gt_ref, local_sem, zsends, zrecvs, sends, recvs
):
    at, y, z, x, core = place()
    ways = near()
    greet([ways["twin"], ways["x"], ways["y"]] + ways["z"])
    chunks = [(0, a, b) for a, b in own_cuts] + [(1, a, b) for a, b in aim_cuts]
    started = []

    def go(ref, chunk, kind, peer):
        copy = remote(ref, ref, sends, recvs, (chunk, kind), peer)
        copy.start()
        started.append(copy)

    def landed(ref, chunk, kind):
        remote(ref, ref, sends, recvs, (chunk, kind), ways["x"]).wait_recv()

    def shard(chunk, zz):
        which, a, b = chunks[chunk]
        if which == 0:
            return gs_ref.at[y, zz, x, core, :, pl.ds(a, b - a)]
        return gt_ref.at[zz, x, core, :, pl.ds(a, b - a)]

    def column(chunk, yy, xx, cc):
        which, a, b = chunks[chunk]
        if which == 0:
            return gs_ref.at[yy, :, xx, cc, :, pl.ds(a, b - a)]
        return gt_ref.at[:, xx, cc, :, pl.ds(a, b - a)]

    def half_column(chunk, yy, xx, cc, half):
        which, a, b = chunks[chunk]
        return gs_ref.at[yy, pl.ds(2 * half, 2), xx, cc, :, pl.ds(a, b - a)]

    own = []
    for k, (which, a, b) in enumerate(chunks):
        source = (ps_ref, pt_ref)[which].at[:, pl.ds(a, b - a)]
        copy = pltpu.make_async_copy(source, shard(k, z), local_sem.at[k])
        copy.start()
        own.append(copy)
        for step in range(3):
            copy = remote(source, shard(k, z), zsends, zrecvs, (k, step), ways["z"][step])
            copy.start()
            started.append(copy)
    for k, (which, a, b) in enumerate(chunks):
        for step in range(3):
            came = shard(k, (z + 3 - step) % 4)
            remote(came, came, zsends, zrecvs, (k, step), ways["x"]).wait_recv()
        own[k].wait()
        go(column(k, y, x, core), k, 0, ways["x"])
        if which == 0:
            go(column(k, y, x, core), k, 1, ways["y"])
        go(column(k, y, x, core), k, 2, ways["twin"])
    for k, (which, a, b) in enumerate(chunks):
        landed(column(k, y, 1 - x, core), k, 0)
        if which == 0:
            go(half_column(k, y, 1 - x, core, 0), k, 3, ways["y"])
        go(column(k, y, 1 - x, core), k, 4, ways["twin"])
        if which == 0:
            landed(column(k, 1 - y, x, core), k, 1)
            go(half_column(k, 1 - y, x, core, 1), k, 5, ways["x"])
            go(column(k, 1 - y, x, core), k, 6, ways["twin"])
    for k, (which, a, b) in enumerate(chunks):
        if which == 0:
            landed(half_column(k, 1 - y, 1 - x, core, 0), k, 3)
            go(half_column(k, 1 - y, 1 - x, core, 0), k, 7, ways["twin"])
            landed(half_column(k, 1 - y, 1 - x, core, 1), k, 5)
            go(half_column(k, 1 - y, 1 - x, core, 1), k, 8, ways["twin"])
    for k, (which, a, b) in enumerate(chunks):
        landed(column(k, y, x, 1 - core), k, 2)
        landed(column(k, y, 1 - x, 1 - core), k, 4)
        if which == 0:
            landed(column(k, 1 - y, x, 1 - core), k, 6)
            landed(half_column(k, 1 - y, 1 - x, 1 - core, 0), k, 7)
            landed(half_column(k, 1 - y, 1 - x, 1 - core, 1), k, 8)
    for copy in started:
        copy.wait_send()


def gather_call(ps, pt, number):
    lines, wide = ps.shape
    own_cuts = tuple((wide * i // 6, wide * (i + 1) // 6) for i in range(6))
    aim_cuts = tuple((wide * i // 6, wide * (i + 1) // 6) for i in range(6))
    count = len(own_cuts) + len(aim_cuts)
    sem = pltpu.SemaphoreType.DMA
    return pl.pallas_call(
        partial(gather_kernel, own_cuts, aim_cuts),
        name="gather_weights",
        out_shape=[
            shape_of(2, 4, 2, 2, lines, wide, kind=low), shape_of(4, 2, 2, lines, wide, kind=low)
        ],
        in_specs=[VMEM_SPEC] * 2,
        out_specs=[ANY_SPEC] * 2,
        scratch_shapes=[
            sem((count,)), sem((count, 3)), sem((count, 3)), sem((count, 9)), sem((count, 9))
        ],
        compiler_params=pltpu.CompilerParams(
            vmem_limit_bytes=LIMIT, collective_id=number, has_side_effects=True
        ),
    )(ps, pt)


def split_kernels(
    tokens,
    teacher_tokens,
    cotangent,
    lengths,
    masked,
    attn_weight,
    out_weight,
    up_weight,
    down_weight,
    attn_first,
    out_first,
    up_first,
    down_first,
    attn_second,
    out_second,
    up_second,
    down_second,
    vectors,
    vector_first,
    vector_second,
    teacher_attn,
    teacher_out,
    teacher_up,
    teacher_down,
    teacher_vectors,
):
    seq_count, length, width = tokens.shape
    rows = length // 2
    y = lax.axis_index("mp")
    weights = (attn_weight, out_weight, up_weight, down_weight)
    x, aim_x = tokens[0], teacher_tokens[0]
    gs, gt = gather_call(
        shard_pack(*weights).astype(low),
        shard_pack(teacher_attn, teacher_out, teacher_up, teacher_down),
        0,
    )
    wide = gs.shape[-1]
    w, aim_w = gs.reshape(2, width, wide), gt.reshape(width, wide)
    vec = vectors.reshape(-1, width)
    bias = jnp.broadcast_to(
        jnp.where(jnp.arange(length) < lengths[0], 0.0, masked_score)[:, None], (length, LOG_PAIR)
    )
    aimed = teacher_call(
        aim_x, aim_w, teacher_vectors.astype(f32).reshape(-1, width), bias, masked[0][:, None], 1
    )
    q, k, v, a, af, logs, r1, z, u, r2, out = forward_call(x, w, vec, bias)
    cot = lax.dynamic_slice_in_dim(cotangent[0], y * rows, rows, 0)
    grad_feed, ga, g1, sums_feed = feed_back_call(
        out, cot, aimed, masked, r1, r2, z, u, a, w, vec
    )
    grad_attn, input_grad, student, sums_attn = attend_back_call(
        x, q, k, v, bias, logs, af, ga, g1, out, w, 2
    )

    def upright(group):
        return (group[0], group[1].T, group[2], group[3].T)

    outs = finish_call(
        grad_attn.reshape(gs.shape[:-1] + (grad_attn.shape[-1],)),
        grad_feed.reshape(gs.shape),
        sums_feed + sums_attn,
        vec,
        vector_first.reshape(-1, width),
        vector_second.reshape(-1, width),
        upright(weights),
        upright((attn_first, out_first, up_first, down_first)),
        upright((attn_second, out_second, up_second, down_second)),
        3,
    )
    norms = outs[15]
    return (
        student[None],
        input_grad[None],
        *upright(outs[:4]),
        *upright(outs[4:8]),
        *upright(outs[8:12]),
        *(value.reshape(-1) for value in outs[12:15]),
        norms[:2, :6],
        norms[2, :6],
    )


def solution(mesh):
    local = split_kernels if dict(mesh.shape) == {"dp": 16, "mp": 2} else split_rows
    return jax.shard_map(
        local,
        mesh=mesh,
        in_specs=(
            P("dp", None, None),
            P("dp", None, None),
            P("dp", None, None),
            P("dp"),
            P("dp", None),
            P(None, "dp", "mp"),
            P("mp", "dp"),
            P("dp", "mp"),
            P("mp", "dp"),
            P(None, "dp", "mp"),
            P("mp", "dp"),
            P("dp", "mp"),
            P("mp", "dp"),
            P(None, "dp", "mp"),
            P("mp", "dp"),
            P("dp", "mp"),
            P("mp", "dp"),
            P(),
            P(),
            P(),
            P(None, "dp", "mp"),
            P("mp", "dp"),
            P("dp", "mp"),
            P("mp", "dp"),
            P(),
        ),
        out_specs=(
            P("dp", None, None),
            P("dp", None, None),
            P(None, "dp", "mp"),
            P("mp", "dp"),
            P("dp", "mp"),
            P("mp", "dp"),
            P(None, "dp", "mp"),
            P("mp", "dp"),
            P("dp", "mp"),
            P("mp", "dp"),
            P(None, "dp", "mp"),
            P("mp", "dp"),
            P("dp", "mp"),
            P("mp", "dp"),
            P(),
            P(),
            P(),
            P(),
            P(),
        ),
        check_vma=False,
    )
```

time: 840 us -> 490 us (0.58)
  Pallas kernels: 0 us -> 451 us
  waiting for transfers between devices: 367 us -> 0 us
  matrix products: 214 us -> 0 us
  local copies, waits for them, and re-layouts: 108 us -> 29.5 us
  other arithmetic: 75.8 us -> 4.3 us
  blocking collectives: 40.7 us -> 0 us
  between operations: 19.3 us -> 1.97 us
    pallas_call x0 -> x6, Pallas kernels: none -> 451 us  [the longest x1 130 us: gather_call(): pl.pallas_call(partial(gather_kernel, own_cuts, aim_cuts), name='gather_w...]
    dot_general x108 -> x0, matrix products: 211 us -> none  [the longest x32 62.2 us: dot_nt(): lax.dot_general(left, right, (((1,), (1,)), ((), ())), preferred_element_...]
    reduce_scatter x1 -> x0, waiting for transfers between devices: 154 us -> none  [split_rows(): lax.psum_scatter(packed_grad, ('mp', 'dp'), scatter_dimension=0, tiled=True)]
    all_gather x4 -> x0, waiting for transfers between devices: 143 us -> none  [the longest x1 78.9 us: split_rows(): lax.all_gather(shard_pack(attn_weight, out_weight, up_weight, down_weight...]
    psum x2 -> x0, waiting for transfers between devices: 45 us -> none  [the longest x1 24.3 us: split_rows(): lax.psum(dot_nt(flat_of(t_mixed), teacher[:, cuts[3]:cuts[4]]), 'mp')]
    psum x1 -> x0, blocking collectives: 40.7 us -> none  [lamb_update(): lax.psum((matrix_squares(*weights), matrix_squares(*steps), vector_grad),...]
    ppermute x2 -> x0, waiting for transfers between devices: 24.6 us -> none  [row_sum(): came = lax.ppermute(other, 'mp', [(0, 1), (1, 0)])]
    reduce_sum x30 -> x0, other arithmetic: 22.5 us -> none  [the longest x12 6.78 us: head_forward(): row_total = jnp.sum(exponent, -1, keepdims=True)]
  transfers between devices with their start and end apart: 9 -> 0, of which waited for: 6 -> 0; matrix products, arithmetic and copies ran while one was open for 11% -> 0% of each run, Pallas kernels for 0% -> 0%
where the time goes in v2:
time: 490 us; the launch traced here: 486 us
  Pallas kernels  451 us (92%)
  local copies, waits for them, and re-layouts  29.5 us (6%)
    pallas_call x1, Pallas kernels, gather_call(): pl.pallas_call(partial(gather_kernel, own_cuts, aim_cuts), name='gather_w...  130 us
    pallas_call x1, Pallas kernels, finish_call(): pl.pallas_call(partial(finish_kernel, chunks), name='sum_and_update', out...  129 us
    pallas_call x1, Pallas kernels, attend_back_call(): pl.pallas_call(attend_back_kernel, name='attention_backward', out_shape=[...  84.8 us
    pallas_call x1, Pallas kernels, forward_call(): pl.pallas_call(forward_kernel, name='student_forward', out_shape=[shape_o...  40 us
    pallas_call x1, Pallas kernels, teacher_call(): pl.pallas_call(teacher_kernel, name='teacher_forward', out_shape=shape_of...  34.3 us
    pallas_call x1, Pallas kernels, feed_back_call(): pl.pallas_call(feed_back_kernel, name='feed_backward', out_shape=[shape_o...  32.4 us
    unnamed x74, local copies, waits for them, and re-layouts  17.6 us

profile of v2, /device:TPU:0, one launch (start us, length us, event | category | flops | bytes accessed | tf_op | source)
XLA Modules:
  0.0 486.5 jit_solution(3621283691291446374)
XLA Ops:
  0.7 0.0 copy-start
  0.7 0.0 copy-start.4
  0.7 0.9 bitcast_dynamic-update-slice_fusion.4
  1.6 0.8 bitcast_dynamic-update-slice_fusion.3
  2.4 0.8 bitcast_dynamic-update-slice_fusion.2
  3.2 0.8 bitcast_dynamic-update-slice_fusion.1
  4.0 0.9 constant_dynamic-update-slice_fusion
  4.9 1.0 convert.21
  5.9 0.9 convert_dynamic-update-slice_fusion.2
  6.8 1.0 convert_dynamic-update-slice_fusion.1
  7.8 0.0 copy-start.6
  7.9 0.7 copy-done.5
  8.6 0.1 copy-done.6
  8.7 130.0 %gather_weights.1 = (bf16[2,4,2,2,48,4608]{5,4,3,2,1,0:T(8,128)(2,1)}, bf16[4,2,2,48,4608]{4,3,2,1,0:T(8,128)(2,1)}) custom-call(bf16[48,4608]{1,0:T(8,128)(2,1)} %copy-done.6, bf16[48,4608]{1,0:T(8,128)(2,1)} %copy-done.5), custom_call_target="tpu_custom_call" | custom-call | tf_op jit(solution)/shard_map/gather_weights/pallas_call | solution.py:1214
  138.8 0.6 reshape.80.vec_ref
  140.1 1.0 broadcast_in_dim.22.bias_ref
  141.1 40.0 %student_forward.1 = (bf16[512,768]{1,0:T(8,128)(2,1)}, bf16[1024,768]{1,0:T(8,128)(2,1)}, bf16[1024,768]{1,0:T(8,128)(2,1)}, bf16[512,768]{1,0:T(8,128)(2,1)}, ...) custom-call(bf16[1024,768]{1,0:T(8,128)(2,1)} %bitcast.56, ...), custom_call_target="tpu_custom_call" | custom-call | tf_op jit(solution)/shard_map/student_forward/pallas_call | solution.py:569
  181.1 0.9 dynamic-slice_bitcast_fusion.cot_ref
  182.1 0.7 reshape.92.vec_ref
  182.8 0.7 copy.44.places_ref
  183.5 34.3 %teacher_forward.1.aimed_ref = f32[128,768]{1,0:T(8,128)} custom-call(bf16[1024,768]{1,0:T(8,128)(2,1)} %bitcast.60, bf16[768,4608]{1,0:T(8,128)(2,1)} %bitcast.55, f32[12,768]{1,0:T(8,128)} %reshape.92.vec_ref, f32[1024,128]{1,0:T(8,128)} %broadcast_in_dim.22.bias_ref, s32[128,1]{1,0:T(8,128)} %copy.44.places_ref), custom_call_target="tpu_custom_call" | custom-call | tf_op jit(solution)/shard_map/teacher_forward/pallas_call | solution.py:648
  217.8 32.4 %feed_backward.1 = (bf16[2,768,4608]{2,1,0:T(8,128)(2,1)}, bf16[512,768]{1,0:T(8,128)(2,1)}, f32[512,768]{1,0:T(8,128)}, f32[12,768]{1,0:T(8,128)}) custom-call(f32[512,768]{1,0:T(8,128)} %get-tuple-element.62.out_ref, bf16[512,768]{1,0:T(8,128)(2,1)} %dynamic-slice_bitcast_fusion.cot_ref, f32[128,768]{1,0:T(8,128)} %teacher_forward.1.aimed_ref, ...), custom_call_target="tpu_custom_call" | custom-call | tf_op jit(solution)/shard_map/feed_backward/pallas_call | solution.py:747
  250.2 0.0 copy-start.22
  250.2 84.8 %attention_backward.1 = (bf16[2,768,1152]{2,1,0:T(8,128)(2,1)}, f32[1024,768]{1,0:T(8,128)}, bf16[1024,768]{1,0:T(8,128)(2,1)}, f32[12,768]{1,0:T(8,128)}) custom-call(bf16[1024,768]{1,0:T(8,128)(2,1)} %bitcast.57, bf16[512,768]{1,0:T(8,128)(2,1)} %get-tuple-element.57.q_ref, bf16[1024,768]{1,0:T(8,128)(2,1)} %get-tuple-element.58.k_ref, ...), custom_call_target="tpu_custom_call" | custom-call | tf_op jit(solution)/shard_map/attention_backward/pallas_call | solution.py:871
  335.0 1.4 add.7.vg_ref
  336.4 0.6 reshape.86.vm_ref
  337.1 0.6 reshape.87.vs_ref
  337.7 129.2 %sum_and_update.1 = (f32[3,48,384]{2,1,0:T(8,128)}, f32[48,384]{1,0:T(8,128)}, f32[48,1536]{1,0:T(8,128)}, f32[48,1536]{1,0:T(8,128)}, f32[3,48,384]{2,1,0:T(8,1...) custom-call(bf16[2,4,2,2,48,1152]{5,4,3,2,1,0:T(8,128)(2,1)} %bitcas, ...), custom_call_target="tpu_custom_call" | custom-call | tf_op jit(solution)/shard_map/sum_and_update/pallas_call | solution.py:1103
  466.9 1.4 reshape.88
  468.3 1.4 reshape.89
  469.7 1.4 reshape.90
  471.1 1.2 slice.33
  472.4 1.2 slice_bitcast_fusion.3
  473.6 1.1 copy.70
  474.7 1.3 copy-done.2
  476.0 1.7 copy.71
  477.7 0.7 copy.72
  478.4 0.6 copy.73
  479.1 0.7 copy.74
  479.8 0.7 copy.75
  480.5 0.7 copy.76
  481.2 0.6 copy.77
  481.8 0.7 copy.78
  482.5 0.7 copy.79
  483.3 0.7 copy.80
  483.9 0.6 copy.81
  484.6 0.7 copy.82
  485.3 0.7 copy.83
  (50 shorter events, 0.2 us)
Async XLA Ops:
  0.7 180.5 %copy-start = (bf16[1,1024,768]{2,1,0:T(8,128)(2,1)S(1)}, bf16[1,1024,768]{2,1,0:T(8,128)(2,1)}, u32[]{:S(2)}) copy-start(bf16[1,1024,768]{2,1,0:T(8,128)(2,1)} %param.27) | copy-start | bytes 4718596
  0.7 7.1 %copy-start.16 = (bf16[1536,48]{0,1:T(8,128)(2,1)S(1)}, bf16[1536,48]{0,1:T(8,128)(2,1)}, u32[]{:S(2)}) copy-start(bf16[1536,48]{0,1:T(8,128)(2,1)} %param.48) | copy-start | bytes 442372
  0.7 7.1 %copy-start.4 = (f32[1536,48]{0,1:T(8,128)S(1)}, f32[1536,48]{0,1:T(8,128)}, u32[]{:S(2)}) copy-start(f32[1536,48]{0,1:T(8,128)} %param.33) | copy-start | bytes 884740
  2.4 136.4 %copy-start.21 = (f32[9216]{0:T(1024)S(1)}, f32[9216]{0:T(1024)}, u32[]{:S(2)}) copy-start(f32[9216]{0:T(1024)} %param.42) | copy-start | bytes 110596
  7.8 0.8 copy-start.5
  7.8 0.9 copy-start.6
  181.1 1.0 copy-start.24
  181.1 1.6 copy-start.25
  250.2 84.8 %copy-start.20 = (f32[12,768]{1,0:T(8,128)S(1)}, f32[12,768]{1,0:T(8,128)}, u32[]{:S(2)}) copy-start(f32[12,768]{1,0:T(8,128)} %get-tuple-element.75) | copy-start | bytes 110596
  250.2 86.3 %copy-start.22 = (f32[9216]{0:T(1024)S(1)}, f32[9216]{0:T(1024)}, u32[]{:S(2)}) copy-start(f32[9216]{0:T(1024)} %param.43) | copy-start | bytes 110596
  250.2 86.9 %copy-start.23 = (f32[9216]{0:T(1024)S(1)}, f32[9216]{0:T(1024)}, u32[]{:S(2)}) copy-start(f32[9216]{0:T(1024)} %param.44) | copy-start | bytes 110596
  337.7 135.9 %copy-start.3 = (bf16[1024,768]{1,0:T(8,128)(2,1)S(1)}, bf16[1024,768]{1,0:T(8,128)(2,1)}, u32[]{:S(2)}) copy-start(bf16[1024,768]{1,0:T(8,128)(2,1)} %get-tuple-element.71) | copy-start | bytes 4718596
  473.6 2.5 copy-start.2
  476.0 1.7 copy-start.15
  476.0 2.4 copy-start.19
  476.0 3.0 copy-start.12
  476.0 3.7 copy-start.11
  477.7 2.8 copy-start.14
  477.7 3.5 copy-start.18
  477.7 4.1 copy-start.10
  477.7 4.8 copy-start.9
  478.4 4.8 copy-start.13
  479.1 4.9 %copy-start.17 = (f32[48,384]{1,0:T(8,128)S(1)}, f32[48,384]{1,0:T(8,128)}, u32[]{:S(2)}) copy-start(f32[48,384]{1,0:T(8,128)} %get-tuple-element.86) | copy-start | bytes 221188
  479.8 4.8 copy-start.8
  480.5 4.8 copy-start.7
  480.5 5.5 %copy-start.1 = (bf16[1,1024,768]{2,1,0:T(8,128)(2,1)S(1)}, bf16[1,1024,768]{2,1,0:T(8,128)(2,1)}, u32[]{:S(2)}) copy-start(bf16[1,1024,768]{2,1,0:T(8,128)(2,1)} %param.27) | copy-start | bytes 4718596
